TPU v7x, 128 devices: a whole 4x4x4 slice. The times are simulated.
128 devices in a mesh: seq: 8 (over z, core), exp: 16 (over y, x).
Axes of the slice: x: 4, y: 4, z: 4, core: 2. Of those that a mesh axis runs over, the one named last changes fastest.
Arguments:
- frames_in: bfloat16 [16, 1024, 768], P('exp', 'seq'), may hold values from -6 to 6
- gain_conv: float32 [768], replicated, may hold values from 0.1 to 1.9
- w_in: bfloat16 [768, 1536], replicated, may hold values from -0.21875 to 0.21875
- dw_kernel: float32 [31, 768], replicated, may hold values from -1 to 1
- w_out: bfloat16 [768, 768], replicated, may hold values from -0.21875 to 0.21875
- gain_moe: float32 [768], replicated, may hold values from 0.1 to 1.9
- w_up: bfloat16 [64, 768, 3072], P('exp', None, 'seq'), may hold values from -0.21875 to 0.21875
- w_down: bfloat16 [64, 3072, 768], P('exp', 'seq'), may hold values from -0.109375 to 0.109375
- route: int32 [16, 1024], P('exp', 'seq'), may hold values from 0 to 63, as said below
- slot: int32 [16, 1024], P('exp', 'seq'), may hold values from 0 to 3, as said below
- grad_out: bfloat16 [16, 1024, 768], P('exp', 'seq'), may hold values from -6 to 6
Outputs:
- block_out: bfloat16 [16, 1024, 768], P('exp', 'seq')
- grad_x: bfloat16 [16, 1024, 768], P('exp', 'seq')
- grad_w_in: float32 [768, 1536], P(('seq', 'exp'))
- grad_dw: float32 [31, 768], P(None, ('seq', 'exp'))
- grad_w_out: float32 [768, 768], P(('seq', 'exp'))
- grad_gain_conv: float32 [768], P(('seq', 'exp'))
- grad_gain_moe: float32 [768], P(('seq', 'exp'))
- grad_w_up: float32 [64, 768, 3072], P('exp', None, 'seq')
- grad_w_down: float32 [64, 3072, 768], P('exp', 'seq')
Inputs may be any that keep to these rules, and one draw needn't show every extreme that they name: `route`: among the 128 frames of one device (an aligned block of the row-major order of all frames) at most 4 name any one expert, and in every draw some expert is named by exactly 4 frames of every device. `slot`: frames of one device that name the same expert have different slots.
All inputs are finite; a program needn't handle non-finite values.
Results may differ from a plain program's by a relative error of at most 0.017.
Values may be sent and summed in bfloat16 or wider, within the bound.
A program may use at most 128 MiB of HBM per device.

v0:
```python
import jax
import jax.numpy as jnp
from jax import lax
from jax.sharding import PartitionSpec as P

NORM_EPSILON = 1e-05


def extended(shard, sides, width):
    for axis, dim in sides:
        size, length = (lax.axis_size(axis), shard.shape[dim])
        up = [(i, (i + 1) % size) for i in range(size - 1)]
        down = [(j, i) for i, j in up]
        last = lax.slice_in_dim(shard, length - width, length, axis=dim)
        initial = lax.slice_in_dim(shard, 0, width, axis=dim)
        before = lax.ppermute(last, axis, up)
        after = lax.ppermute(initial, axis, down)
        shard = jnp.concatenate([before, shard, after], axis=dim)
    return shard


def layer_norm(frame_rows, gain_vec):
    centre = frame_rows - jnp.mean(frame_rows, axis=-1, keepdims=True)
    spread = jnp.mean(centre * centre, axis=-1, keepdims=True)
    return centre * lax.rsqrt(spread + NORM_EPSILON) * gain_vec


def swish_act(values):
    return values * jax.nn.sigmoid(values)


def swish_slope(values):
    logistic = jax.nn.sigmoid(values)
    return logistic + values * logistic * (1.0 - logistic)


def gated_linear(mixed_cols):
    feat_width = mixed_cols.shape[-1] // 2
    return mixed_cols[..., :feat_width] * jax.nn.sigmoid(mixed_cols[..., feat_width:])


def depthwise(padded, kernel, length):
    summed_taps = jnp.zeros(padded.shape[:-2] + (length, padded.shape[-1]), jnp.float32)
    for tap_index in range(kernel.shape[0]):
        summed_taps = summed_taps + kernel[tap_index] * padded[
            ..., tap_index : tap_index + length, :
        ].astype(jnp.float32)
    return summed_taps


def tap_sums(padded, grad_conv, length, tap_count):
    reduce_axes = tuple(range(grad_conv.ndim - 1))
    tap_rows = []
    for tap_index in range(tap_count):
        window = padded[..., tap_index : tap_index + length, :].astype(jnp.float32)
        tap_rows.append(jnp.sum(grad_conv * window, axis=reduce_axes))
    return jnp.stack(tap_rows)


def spread(packed, seq_count):
    copies = jnp.broadcast_to(packed[None], (seq_count,) + packed.shape)
    copies = copies.reshape((seq_count * packed.shape[0],) + packed.shape[1:])
    return lax.all_to_all(copies, ("seq", "exp"), split_axis=0, concat_axis=0, tiled=True)


def collect(partial_value, seq_count):
    sent_rows = partial_value.astype(jnp.bfloat16)
    came_rows = lax.all_to_all(sent_rows, ("seq", "exp"), split_axis=0, concat_axis=0, tiled=True)
    came_rows = came_rows.reshape(
        (seq_count, came_rows.shape[0] // seq_count) + came_rows.shape[1:]
    )
    return jnp.sum(came_rows.astype(jnp.float32), axis=0).astype(jnp.bfloat16)


def per_device(
    frames_in, gain_conv, w_in, dw_kernel, w_out, gain_moe, w_up, w_down, route, slot, grad_out
):
    seq_count = lax.axis_size("seq")
    exp_count = lax.axis_size("exp")
    length = frames_in.shape[1]
    feat_width = frames_in.shape[2]
    local_experts = w_up.shape[0]
    capacity = 2 * length // (local_experts * exp_count)
    slot_count = local_experts * exp_count * capacity
    tap_count = dw_kernel.shape[0]
    half_kernel = tap_count // 2
    dense_scale = (length * seq_count * exp_count) ** (-0.5)
    expert_scale = (seq_count * exp_count * capacity) ** (-0.5)
    source = frames_in[0].astype(jnp.float32)
    normed = layer_norm(source, gain_conv).astype(jnp.bfloat16)
    mixed_cols = jnp.dot(normed, w_in, preferred_element_type=jnp.float32)
    glu_out = gated_linear(mixed_cols).astype(jnp.bfloat16)
    glu_pad = extended(glu_out, (("seq", 0),), half_kernel)
    conv_out = depthwise(glu_pad, dw_kernel, length)
    act_out = swish_act(conv_out).astype(jnp.bfloat16)
    hidden = source + jnp.dot(act_out, w_out, preferred_element_type=jnp.float32)
    moe_in = layer_norm(hidden, gain_moe).astype(jnp.bfloat16)
    column = route[0] * capacity + slot[0]
    slot_table = (column[:, None] == jnp.arange(slot_count, dtype=jnp.int32)[None, :]).astype(
        jnp.bfloat16
    )

    def pack_slots(values):
        packed = jnp.einsum(
            "ls,ld->sd", slot_table, values, preferred_element_type=jnp.float32
        ).astype(jnp.bfloat16)
        return packed.reshape(exp_count, slot_count // exp_count, feat_width)

    def unpack_slots(values):
        return jnp.dot(
            slot_table, values.reshape(slot_count, feat_width), preferred_element_type=jnp.float32
        )

    expert_rows = spread(pack_slots(moe_in), seq_count)
    senders = expert_rows.shape[0]
    expert_rows = expert_rows.reshape(senders, local_experts, capacity, feat_width)
    pre_act = jnp.einsum("recd,edf->recf", expert_rows, w_up, preferred_element_type=jnp.float32)
    up_act = swish_act(pre_act).astype(jnp.bfloat16)
    partial_value = jnp.einsum("recf,efd->recd", up_act, w_down, preferred_element_type=jnp.float32)
    expert_out = unpack_slots(
        collect(partial_value.reshape(senders, local_experts * capacity, feat_width), seq_count)
    )
    block_out = (hidden + 0.5 * expert_out).astype(jnp.bfloat16)
    grad_moe = (0.5 * grad_out[0].astype(jnp.float32)).astype(jnp.bfloat16)
    grad_rows = spread(pack_slots(grad_moe), seq_count).reshape(
        senders, local_experts, capacity, feat_width
    )
    slope_back = jnp.einsum("recd,efd->recf", grad_rows, w_down, preferred_element_type=jnp.float32)
    grad_pre = (slope_back * swish_slope(pre_act)).astype(jnp.bfloat16)
    grad_w_down = (
        jnp.einsum("recf,recd->efd", up_act, grad_rows, preferred_element_type=jnp.float32)
        * expert_scale
    )
    grad_w_up = (
        jnp.einsum("recd,recf->edf", expert_rows, grad_pre, preferred_element_type=jnp.float32)
        * expert_scale
    )
    back_part = jnp.einsum("recf,edf->recd", grad_pre, w_up, preferred_element_type=jnp.float32)
    grad_moe_in = unpack_slots(
        collect(back_part.reshape(senders, local_experts * capacity, feat_width), seq_count)
    )
    _, pull_back = jax.vjp(layer_norm, hidden, gain_moe)
    back_hidden, gain_moe_term = pull_back(grad_moe_in)
    grad_hidden = grad_out[0].astype(jnp.float32) + back_hidden
    hidden_back = grad_hidden.astype(jnp.bfloat16)
    grad_w_out = (
        jnp.einsum("ld,le->de", act_out, hidden_back, preferred_element_type=jnp.float32)
        * dense_scale
    )
    grad_conv = (
        jnp.einsum("le,de->ld", hidden_back, w_out, preferred_element_type=jnp.float32)
        * swish_slope(conv_out)
    ).astype(jnp.bfloat16)
    conv_pad = extended(grad_conv, (("seq", 0),), half_kernel)
    grad_glu = depthwise(conv_pad, dw_kernel[::-1], length)
    grad_dw = tap_sums(glu_pad, grad_conv.astype(jnp.float32), length, tap_count) * dense_scale
    _, pull_glu = jax.vjp(gated_linear, mixed_cols)
    grad_mixed = pull_glu(grad_glu)[0].astype(jnp.bfloat16)
    grad_w_in = (
        jnp.einsum("ld,le->de", normed, grad_mixed, preferred_element_type=jnp.float32)
        * dense_scale
    )
    grad_normed = jnp.einsum("le,de->ld", grad_mixed, w_in, preferred_element_type=jnp.float32)
    _, pull_input = jax.vjp(layer_norm, source, gain_conv)
    back_source, gain_conv_term = pull_input(grad_normed)
    grad_x = (grad_hidden + back_source).astype(jnp.bfloat16)
    shared = (
        lax.psum_scatter(grad_w_in, ("seq", "exp"), scatter_dimension=0, tiled=True),
        lax.psum_scatter(grad_dw, ("seq", "exp"), scatter_dimension=1, tiled=True),
        lax.psum_scatter(grad_w_out, ("seq", "exp"), scatter_dimension=0, tiled=True),
        lax.psum_scatter(
            gain_conv_term * dense_scale, ("seq", "exp"), scatter_dimension=0, tiled=True
        ),
        lax.psum_scatter(
            gain_moe_term * dense_scale, ("seq", "exp"), scatter_dimension=0, tiled=True
        ),
    )
    return (
        block_out[None],
        grad_x[None],
        shared[0],
        shared[1],
        shared[2],
        shared[3],
        shared[4],
        grad_w_up,
        grad_w_down,
    )


def solution(mesh):
    return jax.shard_map(
        per_device,
        mesh=mesh,
        in_specs=(
            P("exp", "seq", None),
            P(),
            P(),
            P(),
            P(),
            P(),
            P("exp", None, "seq"),
            P("exp", "seq", None),
            P("exp", "seq"),
            P("exp", "seq"),
            P("exp", "seq", None),
        ),
        out_specs=(
            P("exp", "seq", None),
            P("exp", "seq", None),
            P(("seq", "exp"), None),
            P(None, ("seq", "exp")),
            P(("seq", "exp"), None),
            P(("seq", "exp")),
            P(("seq", "exp")),
            P("exp", None, "seq"),
            P("exp", "seq", None),
        ),
        check_vma=False,
    )
```

profile of v0, /device:TPU:1, one launch (start us, length us, event | category | flops | bytes accessed | tf_op | source)
XLA Modules:
  0.0 930.8 jit_solution(15383840426315328041)
XLA Ops:
  11.8 11.9 %all-to-all-start.2 = ((bf16[128,16,768]{2,1,0:T(8,128)(2,1)}), bf16[128,16,768]{2,1,0:T(8,128)(2,1)}, u32[]{:S(2)}, u32[]{:S(2)}) async-start(bf16[128,16,768]{2,1,0:T(8,128)(2,1)} %bitcast.134), calls=%async_computation.2 | async-start | bytes 6291456 | tf_op jit(solution)/shard_map/all_to_all | solution.py:63
  34.6 9.6 %collective-permute-done.1 = bf16[15,768]{1,0:T(8,128)(2,1)S(1)} collective-permute-done((bf16[15,768]{1,0:T(8,128)(2,1)S(1)}, bf16[15,768]{1,0:T(8,128)(2,1)S(1)}, u32[]{:S(2)}, u32[]{:S(2)}) %collective-permute-start.1) | collective-permute-done | bytes 23072 | tf_op jit(solution)/shard_map/ppermute | solution.py:17
  48.5 15.8 %all-to-all-done.2 = bf16[128,16,768]{2,1,0:T(8,128)(2,1)} async-done(((bf16[128,16,768]{2,1,0:T(8,128)(2,1)}), bf16[128,16,768]{2,1,0:T(8,128)(2,1)}, u32[]{:S(2)}, u32[]{:S(2)}) %all-to-all-start.2) | async-done | bytes 3145760 | tf_op jit(solution)/shard_map/all_to_all | solution.py:63
  66.2 9.0 all-to-all-start
  75.2 4.6 copy.42
  79.9 35.8 %all-to-all-done = bf16[128,16,768]{2,1,0:T(8,128)(2,1)} async-done(((bf16[128,16,768]{2,1,0:T(8,128)(2,1)}), bf16[128,16,768]{2,1,0:T(8,128)(2,1)}, u32[]{:S(2)}, u32[]{:S(2)}) %all-to-all-start) | async-done | bytes 3145760 | tf_op jit(solution)/shard_map/all_to_all | solution.py:63
  130.8 5.6 all-to-all-start.3
  151.4 25.5 %all-to-all-done.3 = bf16[128,16,768]{2,1,0:T(8,128)(2,1)} async-done(((bf16[128,16,768]{2,1,0:T(8,128)(2,1)}), bf16[128,16,768]{2,1,0:T(8,128)(2,1)}, u32[]{:S(2)}, u32[]{:S(2)}) %all-to-all-start.3) | async-done | bytes 3145760 | tf_op jit(solution)/shard_map/all_to_all | solution.py:68
  176.9 5.2 all-to-all-start.1
  196.4 6.3 collective-permute-done.3
  208.9 341.4 %fusion.206 = (f32[8,1536]{1,0:T(8,128)}, f32[8,768]{1,0:T(8,128)}) fusion(f32[768,1536]{1,0:T(8,128)} %convolution_multiply_fusion, f32[768,768]{1,0:T(8,128)S(1)} %copy-done.8), kind=kCustom, calls=%all-reduce-scatter.2 | all-reduce-scatter fusion | flops 2359297 | bytes 7151616
  554.8 4.7 collective-permute-start.64
  566.7 8.6 collective-permute-start.62
  575.3 28.8 %collective-permute-start.61 = (f32[8,768]{1,0:T(8,128)}, f32[8,768]{1,0:T(8,128)S(1)}, u32[]{:S(2)}, u32[]{:S(2)}) collective-permute-start(f32[8,768]{1,0:T(8,128)} %get-tuple-element.107), channel_id=1, source_target_pairs={{0,26},{1,27},{2,28},{3,29},{4,30},{5,31},{6,32},{7,33},{8,34},{9,... | collective-permute-start | bytes 73736
  616.7 4.7 collective-permute-start.54
  673.8 4.9 collective-permute-start.38
  693.9 5.3 collective-permute-start.30
  736.2 63.7 %all-reduce.9 = (f32[768]{0:T(1024)S(1)}, f32[768]{0:T(1024)S(1)}) all-reduce(f32[768]{0:T(1024)S(1)} %get-tuple-element.123, f32[768]{0:T(1024)S(1)} %get-tuple-element.122), channel_id=5, replica_groups=mesh['seq'=8,'exp'=16] {'seq','exp'}, use_global_device_ids=true, to_apply=%region_45.0.clone | all-reduce | flops 1536 | bytes 12288
  801.1 27.9 %concatenate.75 = f32[262,768]{1,0:T(8,128)S(1)} concatenate(f32[6,768]{1,0:T(8,128)} %copy-done.87, f32[8,768]{1,0:T(8,128)} %collective-permute-done.66, f32[8,768]{1,0:T(8,128)} %collective-permute-done.65, f32[8,768]{1,0:T(8,128)} %collective-permute-done.64, f32[8,768]{1,0:T(8,128)} %copy-done.88, f32[8,768]{1,0:T(8,128)} %copy-done.89, f32[8,768]{1,0:T(8,128)} %copy-done.90, ...), dimensions={0} | concatenate | bytes 1609728
  829.1 4.7 collective-permute-start.13
  833.8 4.2 collective-permute-start.12
  838.0 4.2 collective-permute-start.11
  855.1 5.5 collective-permute-start.6
  872.5 49.6 %concatenate.74 = f32[262,1536]{1,0:T(8,128)} concatenate(f32[6,1536]{1,0:T(8,128)} %copy-done.27, f32[8,1536]{1,0:T(8,128)} %collective-permute-done.34, f32[8,1536]{1,0:T(8,128)} %collective-permute-done.33, f32[8,1536]{1,0:T(8,128)} %collective-permute-done.32, f32[8,1536]{1,0:T(8,128)} %collective-permute-done.31, f32[8,1536]{1,0:T(8,128)} %collective-permute-done.30, ...), dimensions={0} | concatenate | bytes 3219456
  (470 shorter events, 226.4 us)
Async XLA Ops:
  11.8 52.5 %all-to-all-start.2 = ((bf16[128,16,768]{2,1,0:T(8,128)(2,1)}), bf16[128,16,768]{2,1,0:T(8,128)(2,1)}, u32[]{:S(2)}, u32[]{:S(2)}) async-start(bf16[128,16,768]{2,1,0:T(8,128)(2,1)} %bitcast.134), calls=%async_computation.2 | async-start | bytes 6291456 | tf_op jit(solution)/shard_map/all_to_all | solution.py:63
  66.2 49.4 %all-to-all-start = ((bf16[128,16,768]{2,1,0:T(8,128)(2,1)}), bf16[128,16,768]{2,1,0:T(8,128)(2,1)}, u32[]{:S(2)}, u32[]{:S(2)}) async-start(bf16[128,16,768]{2,1,0:T(8,128)(2,1)} %bitcast.135), calls=%async_computation | async-start | bytes 6291456 | tf_op jit(solution)/shard_map/all_to_all | solution.py:63
  130.8 46.1 %all-to-all-start.3 = ((bf16[128,16,768]{2,1,0:T(8,128)(2,1)}), bf16[128,16,768]{2,1,0:T(8,128)(2,1)}, u32[]{:S(2)}, u32[]{:S(2)}) async-start(bf16[128,16,768]{2,1,0:T(8,128)(2,1)} %copy.43), calls=%async_computation.3 | async-start | bytes 6291456 | tf_op jit(solution)/shard_map/all_to_all | solution.py:68
  176.9 462.3 %all-to-all-start.1 = ((bf16[128,16,768]{2,1,0:T(8,128)(2,1)}), bf16[128,16,768]{2,1,0:T(8,128)(2,1)}, u32[]{:S(2)}, u32[]{:S(2)}) async-start(bf16[128,16,768]{2,1,0:T(8,128)(2,1)} %copy.39), calls=%async_computation.1 | async-start | bytes 6291456 | tf_op jit(solution)/shard_map/all_to_all | solution.py:68
  182.2 684.0 %all-reduce.13.cloned.1.call-start = ((), (), s32[]{:S(2)}) async-start(), calls=%async_computation.4 | async-start | bytes 196608
  551.1 24.2 %collective-permute-start.66 = (f32[8,768]{1,0:T(8,128)}, f32[8,768]{1,0:T(8,128)}, u32[]{:S(2)}, u32[]{:S(2)}) collective-permute-start(f32[8,768]{1,0:T(8,128)} %get-tuple-element.107), channel_id=1, source_target_pairs={{0,31},{1,32},{2,33},{3,34},{4,35},{5,36},{6,37},{7,38},{8,39},{9,... | collective-permute-start | bytes 73736
  553.0 51.1 %collective-permute-start.65 = (f32[8,768]{1,0:T(8,128)}, f32[8,768]{1,0:T(8,128)}, u32[]{:S(2)}, u32[]{:S(2)}) collective-permute-start(f32[8,768]{1,0:T(8,128)} %get-tuple-element.107), channel_id=1, source_target_pairs={{0,30},{1,31},{2,32},{3,33},{4,34},{5,35},{6,36},{7,37},{8,38},{9,... | collective-permute-start | bytes 73736
  554.8 50.6 %collective-permute-start.64 = (f32[8,768]{1,0:T(8,128)}, f32[8,768]{1,0:T(8,128)}, u32[]{:S(2)}, u32[]{:S(2)}) collective-permute-start(f32[8,768]{1,0:T(8,128)} %get-tuple-element.107), channel_id=1, source_target_pairs={{0,29},{1,30},{2,31},{3,32},{4,33},{5,34},{6,35},{7,36},{8,37},{9,... | collective-permute-start | bytes 73736
  562.4 46.7 %collective-permute-start.63 = (f32[8,768]{1,0:T(8,128)}, f32[8,768]{1,0:T(8,128)S(1)}, u32[]{:S(2)}, u32[]{:S(2)}) collective-permute-start(f32[8,768]{1,0:T(8,128)} %get-tuple-element.107), channel_id=1, source_target_pairs={{0,28},{1,29},{2,30},{3,31},{4,32},{5,33},{6,34},{7,35},{8,36},{9,... | collective-permute-start | bytes 73736
  566.7 44.4 %collective-permute-start.62 = (f32[8,768]{1,0:T(8,128)}, f32[8,768]{1,0:T(8,128)S(1)}, u32[]{:S(2)}, u32[]{:S(2)}) collective-permute-start(f32[8,768]{1,0:T(8,128)} %get-tuple-element.107), channel_id=1, source_target_pairs={{0,27},{1,28},{2,29},{3,30},{4,31},{5,32},{6,33},{7,34},{8,35},{9,... | collective-permute-start | bytes 73736
  575.3 37.6 %collective-permute-start.61 = (f32[8,768]{1,0:T(8,128)}, f32[8,768]{1,0:T(8,128)S(1)}, u32[]{:S(2)}, u32[]{:S(2)}) collective-permute-start(f32[8,768]{1,0:T(8,128)} %get-tuple-element.107), channel_id=1, source_target_pairs={{0,26},{1,27},{2,28},{3,29},{4,30},{5,31},{6,32},{7,33},{8,34},{9,... | collective-permute-start | bytes 73736
  614.8 18.0 %collective-permute-start.55 = (f32[8,768]{1,0:T(8,128)}, f32[8,768]{1,0:T(8,128)}, u32[]{:S(2)}, u32[]{:S(2)}) collective-permute-start(f32[8,768]{1,0:T(8,128)} %get-tuple-element.107), channel_id=1, source_target_pairs={{0,20},{1,21},{2,22},{3,23},{4,24},{5,25},{6,26},{7,27},{8,28},{9,... | collective-permute-start | bytes 73736
  616.7 19.9 %collective-permute-start.54 = (f32[8,768]{1,0:T(8,128)}, f32[8,768]{1,0:T(8,128)}, u32[]{:S(2)}, u32[]{:S(2)}) collective-permute-start(f32[8,768]{1,0:T(8,128)} %get-tuple-element.107), channel_id=1, source_target_pairs={{0,19},{1,20},{2,21},{3,22},{4,23},{5,24},{6,25},{7,26},{8,27},{9,... | collective-permute-start | bytes 73736
  659.0 19.7 %collective-permute-start.42 = (f32[8,768]{1,0:T(8,128)}, f32[8,768]{1,0:T(8,128)S(1)}, u32[]{:S(2)}, u32[]{:S(2)}) collective-permute-start(f32[8,768]{1,0:T(8,128)} %get-tuple-element.107), channel_id=1, source_target_pairs={{0,7},{1,8},{2,9},{3,10},{4,11},{5,12},{6,13},{7,14},{8,15},{9,16}... | collective-permute-start | bytes 73736
  662.1 18.6 %collective-permute-start.41 = (f32[8,768]{1,0:T(8,128)}, f32[8,768]{1,0:T(8,128)S(1)}, u32[]{:S(2)}, u32[]{:S(2)}) collective-permute-start(f32[8,768]{1,0:T(8,128)} %get-tuple-element.107), channel_id=1, source_target_pairs={{0,6},{1,7},{2,8},{3,9},{4,10},{5,11},{6,12},{7,13},{8,14},{9,15},... | collective-permute-start | bytes 73736
  724.4 104.6 %collective-permute-start.18 = (f32[8,1536]{1,0:T(8,128)}, f32[8,1536]{1,0:T(8,128)S(1)}, u32[]{:S(2)}, u32[]{:S(2)}) collective-permute-start(f32[8,1536]{1,0:T(8,128)} %get-tuple-element.106), channel_id=1, source_target_pairs={{0,15},{1,16},{2,17},{3,18},{4,19},{5,20},{6,21},{7,22},{8,23},{9,... | collective-permute-start | bytes 147464
  727.5 106.3 %collective-permute-start.17 = (f32[8,1536]{1,0:T(8,128)}, f32[8,1536]{1,0:T(8,128)S(1)}, u32[]{:S(2)}, u32[]{:S(2)}) collective-permute-start(f32[8,1536]{1,0:T(8,128)} %get-tuple-element.106), channel_id=1, source_target_pairs={{0,14},{1,15},{2,16},{3,17},{4,18},{5,19},{6,20},{7,21},{8,22},{9,... | collective-permute-start | bytes 147464
  729.8 108.2 %collective-permute-start.16 = (f32[8,1536]{1,0:T(8,128)}, f32[8,1536]{1,0:T(8,128)S(1)}, u32[]{:S(2)}, u32[]{:S(2)}) collective-permute-start(f32[8,1536]{1,0:T(8,128)} %get-tuple-element.106), channel_id=1, source_target_pairs={{0,13},{1,14},{2,15},{3,16},{4,17},{5,18},{6,19},{7,20},{8,21},{9,... | collective-permute-start | bytes 147464
  731.7 110.5 %collective-permute-start.15 = (f32[8,1536]{1,0:T(8,128)}, f32[8,1536]{1,0:T(8,128)S(1)}, u32[]{:S(2)}, u32[]{:S(2)}) collective-permute-start(f32[8,1536]{1,0:T(8,128)} %get-tuple-element.106), channel_id=1, source_target_pairs={{0,12},{1,13},{2,14},{3,15},{4,16},{5,17},{6,18},{7,19},{8,20},{9,... | collective-permute-start | bytes 147464
  733.7 110.5 %collective-permute-start.14 = (f32[8,1536]{1,0:T(8,128)}, f32[8,1536]{1,0:T(8,128)S(1)}, u32[]{:S(2)}, u32[]{:S(2)}) collective-permute-start(f32[8,1536]{1,0:T(8,128)} %get-tuple-element.106), channel_id=1, source_target_pairs={{0,11},{1,12},{2,13},{3,14},{4,15},{5,16},{6,17},{7,18},{8,19},{9,... | collective-permute-start | bytes 147464
  829.1 18.6 %collective-permute-start.13 = (f32[8,1536]{1,0:T(8,128)}, f32[8,1536]{1,0:T(8,128)S(1)}, u32[]{:S(2)}, u32[]{:S(2)}) collective-permute-start(f32[8,1536]{1,0:T(8,128)} %get-tuple-element.106), channel_id=1, source_target_pairs={{0,10},{1,11},{2,12},{3,13},{4,14},{5,15},{6,16},{7,17},{8,18},{9,... | collective-permute-start | bytes 147464
  842.3 18.4 %collective-permute-start.10 = (f32[8,1536]{1,0:T(8,128)}, f32[8,1536]{1,0:T(8,128)}, u32[]{:S(2)}, u32[]{:S(2)}) collective-permute-start(f32[8,1536]{1,0:T(8,128)} %get-tuple-element.106), channel_id=1, source_target_pairs={{0,7},{1,8},{2,9},{3,10},{4,11},{5,12},{6,13},{7,14},{8,15},{9,16}... | collective-permute-start | bytes 147464
  844.2 18.9 %collective-permute-start.9 = (f32[8,1536]{1,0:T(8,128)}, f32[8,1536]{1,0:T(8,128)}, u32[]{:S(2)}, u32[]{:S(2)}) collective-permute-start(f32[8,1536]{1,0:T(8,128)} %get-tuple-element.106), channel_id=1, source_target_pairs={{0,6},{1,7},{2,8},{3,9},{4,10},{5,11},{6,12},{7,13},{8,14},{9,15},... | collective-permute-start | bytes 147464
  847.7 20.0 %collective-permute-start.8 = (f32[8,1536]{1,0:T(8,128)}, f32[8,1536]{1,0:T(8,128)S(1)}, u32[]{:S(2)}, u32[]{:S(2)}) collective-permute-start(f32[8,1536]{1,0:T(8,128)} %get-tuple-element.106), channel_id=1, source_target_pairs={{0,5},{1,6},{2,7},{3,8},{4,9},{5,10},{6,11},{7,12},{8,13},{9,14},{... | collective-permute-start | bytes 147464
  (174 other events, 3374.3 us)
Sparse Core Ops, SparseCore 0:
  656.6 137.3 all-reduce.12
where the time goes:
time: 942 us; the launch traced here: 931 us
  blocking collectives  405 us (43%)
  starting transfers between devices  243 us (26%)
  local copies, waits for them, and re-layouts  116 us (12%)
  waiting for transfers between devices  98 us (10%)
  matrix products  32.7 us (3%)
  other arithmetic  19.1 us (2%)
  between operations  16.9 us (2%)
    unnamed x2, blocking collectives  405 us
    unnamed x65, starting transfers between devices  200 us
    unnamed x260, local copies, waits for them, and re-layouts  93.6 us
    all_to_all x2, waiting for transfers between devices, spread(): lax.all_to_all(copies, ('seq', 'exp'), split_axis=0, concat_axis=0, tiled...  51.6 us
    all_to_all x2, waiting for transfers between devices, collect(): lax.all_to_all(sent_rows, ('seq', 'exp'), split_axis=0, concat_axis=0, ti...  25.5 us
    all_to_all x2, starting transfers between devices, spread(): lax.all_to_all(copies, ('seq', 'exp'), split_axis=0, concat_axis=0, tiled...  20.9 us
  transfers between devices with their start and end apart: 73, of which 7 were waited for; matrix products, arithmetic and copies ran while one was open for 46% of the time, Pallas kernels for 0%

commit v1 on v0

--- a/solution.py
+++ b/solution.py
@@ -164,16 +164,38 @@
     _, pull_input = jax.vjp(layer_norm, source, gain_conv)
     back_source, gain_conv_term = pull_input(grad_normed)
     grad_x = (grad_hidden + back_source).astype(jnp.bfloat16)
+    devices = seq_count * exp_count
+
+    def by_rows(value):
+        return value.reshape(devices, -1)
+
+    sent = jnp.concatenate(
+        [
+            by_rows(grad_w_in),
+            by_rows(grad_w_out),
+            by_rows(grad_dw.T),
+            by_rows(gain_conv_term * dense_scale),
+            by_rows(gain_moe_term * dense_scale),
+        ],
+        axis=1,
+    ).astype(jnp.bfloat16)
+    width = sent.shape[1]
+    tile_rows = -(-width // 2048) * 16
+    sent = jnp.pad(sent, ((0, 0), (0, tile_rows * 128 - width))).reshape(devices, tile_rows, 128)
+    came = lax.all_to_all(sent, ("seq", "exp"), split_axis=0, concat_axis=0, tiled=True)
+    total = jnp.sum(came.astype(jnp.float32), axis=0).reshape(-1)
+    own = feat_width // devices
+    sizes = (own * 2 * feat_width, own * feat_width, own * tap_count, own, own)
+    parts, start = [], 0
+    for size in sizes:
+        parts.append(total[start : start + size])
+        start += size
     shared = (
-        lax.psum_scatter(grad_w_in, ("seq", "exp"), scatter_dimension=0, tiled=True),
-        lax.psum_scatter(grad_dw, ("seq", "exp"), scatter_dimension=1, tiled=True),
-        lax.psum_scatter(grad_w_out, ("seq", "exp"), scatter_dimension=0, tiled=True),
-        lax.psum_scatter(
-            gain_conv_term * dense_scale, ("seq", "exp"), scatter_dimension=0, tiled=True
-        ),
-        lax.psum_scatter(
-            gain_moe_term * dense_scale, ("seq", "exp"), scatter_dimension=0, tiled=True
-        ),
+        parts[0].reshape(own, 2 * feat_width),
+        parts[2].reshape(own, tap_count).T,
+        parts[1].reshape(own, feat_width),
+        parts[3],
+        parts[4],
     )
     return (
         block_out[None],

time: 942 us -> 328 us (0.35)
  blocking collectives: 405 us -> 0 us
  starting transfers between devices: 243 us -> 50.1 us
  local copies, waits for them, and re-layouts: 116 us -> 79.4 us
  waiting for transfers between devices: 98 us -> 127 us
  between operations: 16.9 us -> 1.9 us
  other arithmetic: 19.1 us -> 31.2 us
    unnamed x2 -> x0, blocking collectives: 405 us -> none
    unnamed x65 -> x0, starting transfers between devices: 200 us -> none
    unnamed x260 -> x164, local copies, waits for them, and re-layouts: 93.6 us -> 13.4 us
    all_to_all x0 -> x1, waiting for transfers between devices: none -> 30.4 us  [per_device(): lax.all_to_all(sent, ('seq', 'exp'), split_axis=0, concat_axis=0, tiled=T...]
    another operation x32, local copies, waits for them, and re-layouts: 3.72 us -> 23.8 us  [tap_sums(): return jnp.stack(tap_rows)]
    reshape x0 -> x6, local copies, waits for them, and re-layouts: none -> 12 us  [the longest x3 10.1 us: by_rows(): return value.reshape(devices, -1)]
    all_to_all x0 -> x1, starting transfers between devices: none -> 10.2 us  [per_device(): lax.all_to_all(sent, ('seq', 'exp'), split_axis=0, concat_axis=0, tiled=T...]
  transfers between devices with their start and end apart: 73 -> 9, of which waited for: 7 -> 5; matrix products, arithmetic and copies ran while one was open for 46% -> 35% of each run, Pallas kernels for 0% -> 0%
where the time goes in v1:
time: 328 us; the launch traced here: 326 us
  waiting for transfers between devices  127 us (39%)
  local copies, waits for them, and re-layouts  79.4 us (24%)
  starting transfers between devices  50.1 us (15%)
  matrix products  36.4 us (11%)
  other arithmetic  31.2 us (10%)
    all_to_all x2, waiting for transfers between devices, spread(): lax.all_to_all(copies, ('seq', 'exp'), split_axis=0, concat_axis=0, tiled...  53.1 us
    all_to_all x2, waiting for transfers between devices, collect(): lax.all_to_all(sent_rows, ('seq', 'exp'), split_axis=0, concat_axis=0, ti...  33 us
    all_to_all x1, waiting for transfers between devices, per_device(): lax.all_to_all(sent, ('seq', 'exp'), split_axis=0, concat_axis=0, tiled=T...  30.4 us
    another operation x32, local copies, waits for them, and re-layouts, tap_sums(): return jnp.stack(tap_rows)  23.8 us
    all_to_all x2, starting transfers between devices, spread(): lax.all_to_all(copies, ('seq', 'exp'), split_axis=0, concat_axis=0, tiled...  19 us
    unnamed x164, local copies, waits for them, and re-layouts  13.4 us
    ppermute x2, waiting for transfers between devices, extended(): after = lax.ppermute(initial, axis, down)  10.6 us
    all_to_all x1, starting transfers between devices, per_device(): lax.all_to_all(sent, ('seq', 'exp'), split_axis=0, concat_axis=0, tiled=T...  10.2 us
  transfers between devices with their start and end apart: 9, of which 5 were waited for; matrix products, arithmetic and copies ran while one was open for 35% of the time, Pallas kernels for 0%

profile of v1, /device:TPU:1, one launch (start us, length us, event | category | flops | bytes accessed | tf_op | source)
XLA Modules:
  0.0 326.1 jit_solution(8499444692463053258)
XLA Ops:
  4.7 11.9 %all-to-all-start.2 = ((bf16[128,16,768]{2,1,0:T(8,128)(2,1)}), bf16[128,16,768]{2,1,0:T(8,128)(2,1)}, u32[]{:S(2)}, u32[]{:S(2)}) async-start(bf16[128,16,768]{2,1,0:T(8,128)(2,1)} %bitcast.140), calls=%async_computation.2 | async-start | bytes 6291456 | tf_op jit(solution)/shard_map/all_to_all | solution.py:63
  20.3 3.7 %collective-permute-start = (bf16[15,768]{1,0:T(8,128)(2,1)S(1)}, bf16[15,768]{1,0:T(8,128)(2,1)S(1)}, u32[]{:S(2)}, u32[]{:S(2)}) collective-permute-start(bf16[15,768]{1,0:T(8,128)(2,1)S(1)} %get-tuple-element.81), channel_id=1, source_target_pairs={{0,16},{16,32},{32,48},{48,64},{64,80},{80,96},{96,112},{1,17},{17... | collective-permute-start | bytes 69128 | tf_op jit(solution)/shard_map/ppermute | solution.py:16
  26.5 10.6 %collective-permute-done.1 = bf16[15,768]{1,0:T(8,128)(2,1)S(1)} collective-permute-done((bf16[15,768]{1,0:T(8,128)(2,1)S(1)}, bf16[15,768]{1,0:T(8,128)(2,1)S(1)}, u32[]{:S(2)}, u32[]{:S(2)}) %collective-permute-start.1) | collective-permute-done | bytes 23072 | tf_op jit(solution)/shard_map/ppermute | solution.py:17
  40.2 17.1 %all-to-all-done.2 = bf16[128,16,768]{2,1,0:T(8,128)(2,1)} async-done(((bf16[128,16,768]{2,1,0:T(8,128)(2,1)}), bf16[128,16,768]{2,1,0:T(8,128)(2,1)}, u32[]{:S(2)}, u32[]{:S(2)}) %all-to-all-start.2) | async-done | bytes 3145760 | tf_op jit(solution)/shard_map/all_to_all | solution.py:63
  59.5 7.1 %all-to-all-start = ((bf16[128,16,768]{2,1,0:T(8,128)(2,1)}), bf16[128,16,768]{2,1,0:T(8,128)(2,1)}, u32[]{:S(2)}, u32[]{:S(2)}) async-start(bf16[128,16,768]{2,1,0:T(8,128)(2,1)} %bitcast.141), calls=%async_computation | async-start | bytes 6291456 | tf_op jit(solution)/shard_map/all_to_all | solution.py:63
  66.6 4.6 %copy.42 = bf16[128,16,768]{2,0,1:T(8,128)(2,1)} copy(bf16[128,16,768]{2,1,0:T(8,128)(2,1)} %all-to-all-done.2) | data formatting | bytes 6291456 | tf_op jit(solution)/shard_map/all_to_all | solution.py:63
  71.2 36.0 %all-to-all-done = bf16[128,16,768]{2,1,0:T(8,128)(2,1)} async-done(((bf16[128,16,768]{2,1,0:T(8,128)(2,1)}), bf16[128,16,768]{2,1,0:T(8,128)(2,1)}, u32[]{:S(2)}, u32[]{:S(2)}) %all-to-all-start) | async-done | bytes 3145760 | tf_op jit(solution)/shard_map/all_to_all | solution.py:63
  118.8 3.4 %copy.43 = bf16[128,16,768]{2,1,0:T(8,128)(2,1)} copy(bf16[128,16,768]{2,0,1:T(8,128)(2,1)S(1)} %bitcast.139) | data formatting | bytes 6291456 | tf_op jit(solution)/shard_map/convert_element_type | solution.py:67
  122.2 4.8 %all-to-all-start.3 = ((bf16[128,16,768]{2,1,0:T(8,128)(2,1)}), bf16[128,16,768]{2,1,0:T(8,128)(2,1)S(1)}, u32[]{:S(2)}, u32[]{:S(2)}) async-start(bf16[128,16,768]{2,1,0:T(8,128)(2,1)} %copy.43), calls=%async_computation.3 | async-start | bytes 6291456 | tf_op jit(solution)/shard_map/all_to_all | solution.py:68
  127.0 4.4 %fusion.12 = bf16[4,128,4,768]{3,1,2,0:T(8,128)(2,1)S(1)} fusion(bf16[4,384,768]{2,1,0:T(8,128)(2,1)} %param.18, f32[4,128,4,384]{3,1,2,0:T(8,128)} %copy-done.21), kind=kOutput, calls=%fused_computation.53 | convolution fusion | flops 1213464576 | bytes 8650752 | tf_op jit(solution)/shard_map/recf,efd->recd/dot_general | solution.py:119
  131.5 3.4 %copy.39 = bf16[128,16,768]{2,1,0:T(8,128)(2,1)} copy(bf16[128,16,768]{2,0,1:T(8,128)(2,1)S(1)} %bitcast.146) | data formatting | bytes 6291456 | tf_op jit(solution)/shard_map/convert_element_type | solution.py:67
  134.9 33.0 %all-to-all-done.3 = bf16[128,16,768]{2,1,0:T(8,128)(2,1)S(1)} async-done(((bf16[128,16,768]{2,1,0:T(8,128)(2,1)}), bf16[128,16,768]{2,1,0:T(8,128)(2,1)S(1)}, u32[]{:S(2)}, u32[]{:S(2)}) %all-to-all-start.3) | async-done | bytes 3145760 | tf_op jit(solution)/shard_map/all_to_all | solution.py:68
  169.6 4.8 %all-to-all-start.1 = ((bf16[128,16,768]{2,1,0:T(8,128)(2,1)}), bf16[128,16,768]{2,1,0:T(8,128)(2,1)S(1)}, u32[]{:S(2)}, u32[]{:S(2)}) async-start(bf16[128,16,768]{2,1,0:T(8,128)(2,1)} %copy.39), calls=%async_computation.1 | async-start | bytes 6291456 | tf_op jit(solution)/shard_map/all_to_all | solution.py:68
  174.4 3.2 reduce_sum.447
  204.3 3.7 %collective-permute-start.2 = (bf16[15,768]{1,0:T(8,128)(2,1)}, bf16[15,768]{1,0:T(8,128)(2,1)}, u32[]{:S(2)}, u32[]{:S(2)}) collective-permute-start(bf16[15,768]{1,0:T(8,128)(2,1)} %get-tuple-element.79), channel_id=1, source_target_pairs={{0,16},{16,32},{32,48},{48,64},{64,80},{80,96},{96,112},{1,17},{17... | collective-permute-start | bytes 69128 | tf_op jit(solution)/shard_map/ppermute | solution.py:16
  210.2 5.5 %stack.127 = f32[31,768]{1,0:T(8,128)} concatenate(f32[1,768]{1,0:T(1,128)} %stack.96, f32[1,768]{1,0:T(1,128)} %stack.97, f32[1,768]{1,0:T(1,128)} %stack.98, f32[1,768]{1,0:T(1,128)} %stack.99, f32[1,768]{1,0:T(1,128)} %stack.100, f32[1,768]{1,0:T(1,128)} %stack.101, f32[1,768]{1,0:T(1,128)} %stack.102, f32[1,768]{1,0:T(1,128)} %stack.103, f32[1,768]{1,0:T(1,128)} %stack.104, ...), dimensions={0} | concatenate | bytes 190464 | tf_op jit(solution)/shard_map/stack | solution.py:57
  228.9 9.2 %fusion.67 = (f32[128,768]{1,0:T(8,128)S(1)}, f32[128,768]{1,0:T(8,128)S(1)}) fusion(f32[128,1536]{1,0:T(8,128)} %copy-done.9, bf16[15,768]{1,0:T(8,128)(2,1)} %collective-permute-done.3, bf16[128,768]{1,0:T(8,128)(2,1)} %copy-done.14, f32[768]{0:T(1024)S(1)} %get-tuple-element.44, f32[768]{0:T(1024)} %copy-done.51, f32[768]{0:T(1024)} %copy-done.60, ...), kind=kLoop, calls=%fused_computation.202 | loop fusion | flops 18579456 | bytes 1910784 | tf_op jit(solution)/shard_map/transpose(jvp())/mul | solution.py:39
  242.7 3.5 %multiply_convert_fusion = bf16[768,1536]{1,0:T(8,128)(2,1)} fusion(f32[128,768]{1,0:T(8,128)} %copy-done.15, f32[128,768]{1,0:T(8,128)} %copy-done.17, bf16[1,128,768]{2,1,0:T(8,128)(2,1)} %param.11, f32[768]{0:T(1024)S(1)} %copy-done.28, f32[128]{0:T(128)S(1)} %copy-done.68, f32[128]{0:T(128)S(1)} %copy-done.65), kind=kOutput, calls=%fused_computation.3 | convolution fusion | flops 305233920 | bytes 3346432 | tf_op jit(solution)/shard_map/ld,le->de/dot_general | solution.py:160
  246.2 5.4 %reshape.169 = bf16[128,9216]{1,0:T(8,128)(2,1)} reshape(bf16[768,1536]{1,0:T(8,128)(2,1)} %multiply_convert_fusion) | data formatting | bytes 4718592 | tf_op jit(solution)/shard_map/reshape | solution.py:170
  251.6 6.7 %concatenate.78 = bf16[128,14022]{1,0:T(8,128)(2,1)} concatenate(bf16[128,9216]{1,0:T(8,128)(2,1)} %reshape.169, bf16[128,4608]{1,0:T(8,128)(2,1)} %reshape.170, bf16[128,186]{1,0:T(8,128)(2,1)} %reshape.171, bf16[128,6]{1,0:T(8,128)(2,1)} %mul.1001, bf16[128,6]{1,0:T(8,128)(2,1)} %mul.1004), dimensions={1} | concatenate | bytes 7179264 | tf_op jit(solution)/shard_map/concatenate | solution.py:172
  264.9 10.2 %all-to-all-start.4 = ((bf16[128,112,128]{2,1,0:T(8,128)(2,1)}), bf16[128,112,128]{2,1,0:T(8,128)(2,1)}, u32[]{:S(2)}, u32[]{:S(2)}) async-start(bf16[128,112,128]{2,1,0:T(8,128)(2,1)} %bitcast.138), calls=%async_computation.4 | async-start | bytes 7340032 | tf_op jit(solution)/shard_map/all_to_all | solution.py:185
  275.1 5.6 %bitcast_multiply_fusion.1 = f32[4,768,384]{2,1,0:T(8,128)} fusion(bf16[128,4,4,768]{3,0,2,1:T(8,128)(2,1)S(1)} %bitcast.137, bf16[128,4,4,384]{3,0,2,1:T(8,128)(2,1)} %copy-done.11), kind=kOutput, calls=%fused_computation.2 | convolution fusion | flops 1209139200 | bytes 9437184 | tf_op jit(solution)/shard_map/recd,recf->edf/dot_general | solution.py:135
  280.7 3.8 %bitcast_multiply_fusion = f32[4,384,768]{2,1,0:T(8,128)} fusion(bf16[128,4,4,768]{3,0,2,1:T(8,128)(2,1)S(1)} %bitcast.145, f32[4,128,4,384]{3,1,2,0:T(8,128)S(1)} %copy-done.22), kind=kOutput, calls=%fused_computation.1 | convolution fusion | flops 1213071360 | bytes 11010048 | tf_op jit(solution)/shard_map/recf,recd->efd/dot_general | solution.py:131
  290.7 30.4 %all-to-all-done.4 = bf16[128,112,128]{2,1,0:T(8,128)(2,1)} async-done(((bf16[128,112,128]{2,1,0:T(8,128)(2,1)}), bf16[128,112,128]{2,1,0:T(8,128)(2,1)}, u32[]{:S(2)}, u32[]{:S(2)}) %all-to-all-start.4) | async-done | bytes 3670048 | tf_op jit(solution)/shard_map/all_to_all | solution.py:185
  (259 shorter events, 92.5 us)
Async XLA Ops:
  0.6 109.4 %copy-start = (bf16[4,768,384]{2,1,0:T(8,128)(2,1)S(1)}, bf16[4,768,384]{2,1,0:T(8,128)(2,1)}, u32[]{:S(2)}) copy-start(bf16[4,768,384]{2,1,0:T(8,128)(2,1)} %param.17) | copy-start | bytes 7077892
  1.5 38.3 %copy-start.69 = (s32[128]{0:T(128)}, s32[128]{0:T(128)S(1)}, u32[]{:S(2)}) copy-start(s32[128]{0:T(128)S(1)} %add_bitcast_fusion) | copy-start | bytes 1540
  4.7 52.5 %all-to-all-start.2 = ((bf16[128,16,768]{2,1,0:T(8,128)(2,1)}), bf16[128,16,768]{2,1,0:T(8,128)(2,1)}, u32[]{:S(2)}, u32[]{:S(2)}) async-start(bf16[128,16,768]{2,1,0:T(8,128)(2,1)} %bitcast.140), calls=%async_computation.2 | async-start | bytes 6291456 | tf_op jit(solution)/shard_map/all_to_all | solution.py:63
  20.3 6.2 %collective-permute-start = (bf16[15,768]{1,0:T(8,128)(2,1)S(1)}, bf16[15,768]{1,0:T(8,128)(2,1)S(1)}, u32[]{:S(2)}, u32[]{:S(2)}) collective-permute-start(bf16[15,768]{1,0:T(8,128)(2,1)S(1)} %get-tuple-element.81), channel_id=1, source_target_pairs={{0,16},{16,32},{32,48},{48,64},{64,80},{80,96},{96,112},{1,17},{17... | collective-permute-start | bytes 69128 | tf_op jit(solution)/shard_map/ppermute | solution.py:16
  24.0 13.1 %collective-permute-start.1 = (bf16[15,768]{1,0:T(8,128)(2,1)S(1)}, bf16[15,768]{1,0:T(8,128)(2,1)S(1)}, u32[]{:S(2)}, u32[]{:S(2)}) collective-permute-start(bf16[15,768]{1,0:T(8,128)(2,1)S(1)} %get-tuple-element.82), channel_id=1, source_target_pairs={{16,0},{32,16},{48,32},{64,48},{80,64},{96,80},{112,96},{17,1},{33... | collective-permute-start | bytes 69128 | tf_op jit(solution)/shard_map/ppermute | solution.py:17
  26.1 33.1 %copy-start.33 = (f32[768]{0:T(1024)}, f32[768]{0:T(1024)S(1)}, u32[]{:S(2)}) copy-start(f32[768]{0:T(1024)S(1)} %get-tuple-element.46) | copy-start | bytes 9220
  26.1 33.1 %copy-start.35 = (f32[768]{0:T(1024)}, f32[768]{0:T(1024)S(1)}, u32[]{:S(2)}) copy-start(f32[768]{0:T(1024)S(1)} %get-tuple-element.47) | copy-start | bytes 9220
  26.1 33.0 %copy-start.36 = (f32[768]{0:T(1024)}, f32[768]{0:T(1024)S(1)}, u32[]{:S(2)}) copy-start(f32[768]{0:T(1024)S(1)} %get-tuple-element.48) | copy-start | bytes 9220
  26.2 33.0 %copy-start.37 = (f32[768]{0:T(1024)}, f32[768]{0:T(1024)S(1)}, u32[]{:S(2)}) copy-start(f32[768]{0:T(1024)S(1)} %get-tuple-element.49) | copy-start | bytes 9220
  26.2 33.0 %copy-start.38 = (f32[768]{0:T(1024)}, f32[768]{0:T(1024)S(1)}, u32[]{:S(2)}) copy-start(f32[768]{0:T(1024)S(1)} %get-tuple-element.50) | copy-start | bytes 9220
  26.2 33.0 %copy-start.39 = (f32[768]{0:T(1024)}, f32[768]{0:T(1024)S(1)}, u32[]{:S(2)}) copy-start(f32[768]{0:T(1024)S(1)} %get-tuple-element.51) | copy-start | bytes 9220
  26.2 33.0 %copy-start.40 = (f32[768]{0:T(1024)}, f32[768]{0:T(1024)S(1)}, u32[]{:S(2)}) copy-start(f32[768]{0:T(1024)S(1)} %get-tuple-element.52) | copy-start | bytes 9220
  26.2 33.0 %copy-start.41 = (f32[768]{0:T(1024)}, f32[768]{0:T(1024)S(1)}, u32[]{:S(2)}) copy-start(f32[768]{0:T(1024)S(1)} %get-tuple-element.53) | copy-start | bytes 9220
  26.2 33.0 %copy-start.42 = (f32[768]{0:T(1024)}, f32[768]{0:T(1024)S(1)}, u32[]{:S(2)}) copy-start(f32[768]{0:T(1024)S(1)} %get-tuple-element.54) | copy-start | bytes 9220
  26.2 33.0 %copy-start.43 = (f32[768]{0:T(1024)}, f32[768]{0:T(1024)S(1)}, u32[]{:S(2)}) copy-start(f32[768]{0:T(1024)S(1)} %get-tuple-element.55) | copy-start | bytes 9220
  26.2 33.0 %copy-start.44 = (f32[768]{0:T(1024)}, f32[768]{0:T(1024)S(1)}, u32[]{:S(2)}) copy-start(f32[768]{0:T(1024)S(1)} %get-tuple-element.56) | copy-start | bytes 9220
  59.5 47.7 %all-to-all-start = ((bf16[128,16,768]{2,1,0:T(8,128)(2,1)}), bf16[128,16,768]{2,1,0:T(8,128)(2,1)}, u32[]{:S(2)}, u32[]{:S(2)}) async-start(bf16[128,16,768]{2,1,0:T(8,128)(2,1)} %bitcast.141), calls=%async_computation | async-start | bytes 6291456 | tf_op jit(solution)/shard_map/all_to_all | solution.py:63
  122.2 45.7 %all-to-all-start.3 = ((bf16[128,16,768]{2,1,0:T(8,128)(2,1)}), bf16[128,16,768]{2,1,0:T(8,128)(2,1)S(1)}, u32[]{:S(2)}, u32[]{:S(2)}) async-start(bf16[128,16,768]{2,1,0:T(8,128)(2,1)} %copy.43), calls=%async_computation.3 | async-start | bytes 6291456 | tf_op jit(solution)/shard_map/all_to_all | solution.py:68
  169.6 93.6 %all-to-all-start.1 = ((bf16[128,16,768]{2,1,0:T(8,128)(2,1)}), bf16[128,16,768]{2,1,0:T(8,128)(2,1)S(1)}, u32[]{:S(2)}, u32[]{:S(2)}) async-start(bf16[128,16,768]{2,1,0:T(8,128)(2,1)} %copy.39), calls=%async_computation.1 | async-start | bytes 6291456 | tf_op jit(solution)/shard_map/all_to_all | solution.py:68
  194.8 34.0 %copy-start.34 = (f32[768]{0:T(1024)S(1)}, f32[768]{0:T(1024)}, u32[]{:S(2)}) copy-start(f32[768]{0:T(1024)} %copy-done.33) | copy-start | bytes 9220
  204.3 24.5 %collective-permute-start.2 = (bf16[15,768]{1,0:T(8,128)(2,1)}, bf16[15,768]{1,0:T(8,128)(2,1)}, u32[]{:S(2)}, u32[]{:S(2)}) collective-permute-start(bf16[15,768]{1,0:T(8,128)(2,1)} %get-tuple-element.79), channel_id=1, source_target_pairs={{0,16},{16,32},{32,48},{48,64},{64,80},{80,96},{96,112},{1,17},{17... | collective-permute-start | bytes 69128 | tf_op jit(solution)/shard_map/ppermute | solution.py:16
  208.0 20.9 %collective-permute-start.3 = (bf16[15,768]{1,0:T(8,128)(2,1)}, bf16[15,768]{1,0:T(8,128)(2,1)}, u32[]{:S(2)}, u32[]{:S(2)}) collective-permute-start(bf16[15,768]{1,0:T(8,128)(2,1)} %get-tuple-element.80), channel_id=1, source_target_pairs={{16,0},{32,16},{48,32},{64,48},{80,64},{96,80},{112,96},{17,1},{33... | collective-permute-start | bytes 69128 | tf_op jit(solution)/shard_map/ppermute | solution.py:17
  264.9 56.2 %all-to-all-start.4 = ((bf16[128,112,128]{2,1,0:T(8,128)(2,1)}), bf16[128,112,128]{2,1,0:T(8,128)(2,1)}, u32[]{:S(2)}, u32[]{:S(2)}) async-start(bf16[128,112,128]{2,1,0:T(8,128)(2,1)} %bitcast.138), calls=%async_computation.4 | async-start | bytes 7340032 | tf_op jit(solution)/shard_map/all_to_all | solution.py:185
  285.7 40.4 %copy-start.1 = (bf16[4,768,384]{2,1,0:T(8,128)(2,1)S(1)}, bf16[4,768,384]{2,1,0:T(8,128)(2,1)}, u32[]{:S(2)}) copy-start(bf16[4,768,384]{2,1,0:T(8,128)(2,1)} %param.17) | copy-start | bytes 7077892
  (66 other events, 967.7 us)

commit v2 on v1

--- a/solution.py
+++ b/solution.py
@@ -1,6 +1,8 @@
 import jax
 import jax.numpy as jnp
 from jax import lax
+from jax.experimental import pallas as pl
+from jax.experimental.pallas import tpu as pltpu
 from jax.sharding import PartitionSpec as P
 
 NORM_EPSILON = 1e-05
@@ -57,19 +59,377 @@
     return jnp.stack(tap_rows)
 
 
-def spread(packed, seq_count):
-    copies = jnp.broadcast_to(packed[None], (seq_count,) + packed.shape)
-    copies = copies.reshape((seq_count * packed.shape[0],) + packed.shape[1:])
-    return lax.all_to_all(copies, ("seq", "exp"), split_axis=0, concat_axis=0, tiled=True)
-
-
-def collect(partial_value, seq_count):
-    sent_rows = partial_value.astype(jnp.bfloat16)
-    came_rows = lax.all_to_all(sent_rows, ("seq", "exp"), split_axis=0, concat_axis=0, tiled=True)
-    came_rows = came_rows.reshape(
-        (seq_count, came_rows.shape[0] // seq_count) + came_rows.shape[1:]
-    )
-    return jnp.sum(came_rows.astype(jnp.float32), axis=0).astype(jnp.bfloat16)
+NZ = 4
+NX = 4
+BF16 = jnp.bfloat16
+F32 = jnp.float32
+MESH = pl.DeviceIdType.MESH
+
+
+def dot_nn(left, right):
+    return lax.dot_general(left, right, (((1,), (0,)), ((), ())), preferred_element_type=F32)
+
+
+def dot_nt(left, right):
+    return lax.dot_general(left, right, (((1,), (1,)), ((), ())), preferred_element_type=F32)
+
+
+def dot_tn(left, right):
+    return lax.dot_general(left, right, (((0,), (0,)), ((), ())), preferred_element_type=F32)
+
+
+def iota(shape, dim):
+    return lax.broadcasted_iota(jnp.int32, shape, dim)
+
+
+def normalise(rows):
+    centre = rows - jnp.mean(rows, axis=-1, keepdims=True)
+    spread = jnp.mean(centre * centre, axis=-1, keepdims=True)
+    scale = lax.rsqrt(spread + NORM_EPSILON)
+    return centre * scale, scale
+
+
+def shift_copies(padded, shifted):
+    shifted[0] = padded[...].astype(F32)
+    for s in range(1, 8):
+        shifted[s, 0:152] = shifted[0, s : s + 152]
+
+
+def conv_taps(shifted, dw, out, flip):
+    for block in range(6):
+        cols = pl.ds(block * 128, 128)
+        total = jnp.zeros((128, 128), F32)
+        for k in range(31):
+            row = 30 - k if flip else k
+            a, s = divmod(k + 1, 8)
+            total = total + dw[row : row + 1, cols] * shifted[s, 8 * a : 8 * a + 128, cols]
+        out[:, cols] = total
+
+
+def fused_kernel(
+    frames, gain_c, w_in, dw, w_out, gain_m, w_up, w_down, route, slot, gout,
+    eo_o, gmi_o, hidden_o, conv_o, glu_o, mixed_o, normed_o, act_o, rows_o, grows_o, up_o, gpre_o,
+    win_v, wout_v, wup_v, wdn_v, load_sem,
+    pt, pk, raw, xp, shifted, y_v, sr, ruf, rdf, ru, rd, fs, gr,
+    pl_s, pl_r, halo_s, halo_r, zs, zr, zfs, zfr, sib_s, sib_r,
+    csib_s, csib_r, cz_s, cz_r, cp_s, cp_r, loc_sem,
+):
+    seq = lax.axis_index("seq")
+    exp = lax.axis_index("exp")
+    z, c = lax.div(seq, 2), lax.rem(seq, 2)
+    y, x = lax.div(exp, 4), lax.rem(exp, 4)
+    zu, zd, zo = lax.rem(z + 1, 4), lax.rem(z + 3, 4), lax.rem(z + 2, 4)
+    up_dev, dn_dev, sib_dev = (zu * 2 + c, exp), (zd * 2 + c, exp), (z * 2 + 1 - c, exp)
+    next_dev, prev_dev = (lax.rem(seq + 1, 8), exp), (lax.rem(seq + 7, 8), exp)
+    offsets = [(dy, dx) for dy in range(4) for dx in range(4)]
+
+    def plane_to(dy, dx):
+        return lax.rem(y + dy, 4), lax.rem(x + dx, 4)
+
+    loads = [
+        pltpu.make_async_copy(src, dst, load_sem.at[i])
+        for i, (src, dst) in enumerate(
+            ((w_in, win_v), (w_out, wout_v), (w_down, wdn_v), (w_up, wup_v))
+        )
+    ]
+    for load in loads:
+        load.start()
+
+    barrier = pltpu.get_barrier_semaphore()
+    partners = [up_dev, dn_dev, next_dev, prev_dev]
+    for dy, dx in offsets[1:]:
+        ty, tx = plane_to(dy, dx)
+        partners.append((seq, ty * 4 + tx))
+    for partner in partners:
+        pl.semaphore_signal(barrier, inc=1, device_id=partner, device_id_type=MESH)
+
+    sent = []
+
+    def send(src, dst, ssem, rsem, dev):
+        copy = pltpu.make_async_remote_copy(
+            src_ref=src, dst_ref=dst, send_sem=ssem, recv_sem=rsem,
+            device_id=dev, device_id_type=MESH,
+        )
+        copy.start()
+        sent.append(copy)
+        return copy
+
+    column = route[...] * 4 + slot[...]
+    pt[...] = (iota((256, 128), 0) == column).astype(F32).astype(BF16)
+
+    def pack(values, t):
+        packed = dot_nn(pt[...], values).astype(BF16)
+        pk[t] = packed.reshape(4, 4, 16, 768)
+
+    def plane_sends(t):
+        own = pltpu.make_async_copy(pk.at[t, y, x], raw.at[t, y, x], loc_sem.at[t])
+        own.start()
+        copies = [own]
+        for i, (dy, dx) in enumerate(offsets):
+            if i == 0:
+                continue
+            ty, tx = plane_to(dy, dx)
+            copies.append(
+                send(pk.at[t, ty, tx], raw.at[t, y, x], pl_s.at[t, i], pl_r.at[t, i],
+                     (seq, ty * 4 + tx))
+            )
+        return copies
+
+    r64 = iota((64, 64), 0)
+    perm = (
+        ((r64 // 4) % 4) * 16 + (r64 // 16) * 4 + r64 % 4 == iota((64, 64), 1)
+    ).astype(F32).astype(BF16)
+
+    def gather_first(t, copies):
+        out = {"up": [], "dn": []}
+        for dy in range(4):
+            for dx in range(4):
+                copy = copies[dy * 4 + dx]
+                if dy + dx == 0:
+                    copy.wait()
+                else:
+                    copy.wait_recv()
+            ry = lax.rem(y + 4 - dy, 4)
+            block = dot_nn(perm, raw[t, ry].reshape(64, 768)).astype(BF16)
+            xp[t, :, seq, ry] = block.reshape(4, 16, 768)
+            ref = xp.at[t, :, seq, ry]
+            out["up"].append(send(ref, ref, zs.at[t, 0, dy], zr.at[t, 0, dy], up_dev))
+            out["dn"].append(send(ref, ref, zs.at[t, 1, dy], zr.at[t, 1, dy], dn_dev))
+        ref = xp.at[t, :, seq]
+        out["sib"] = [send(ref, ref, sib_s.at[t, 0], sib_r.at[t, 0], sib_dev)]
+        return out
+
+    def gather_forward(t, out):
+        lo, hi = zd * 2 + c, zu * 2 + c
+        out["fwd"] = []
+        order = (0, 1, 2, 3)
+        for dy in order:
+            ry = lax.rem(y + 4 - dy, 4)
+            out["up"][dy].wait_recv()
+            if dy < 2:
+                ref = xp.at[t, :, lo, ry]
+                out["fwd"].append(send(ref, ref, zfs.at[t, dy], zfr.at[t, dy], up_dev))
+            out["dn"][dy].wait_recv()
+            if dy >= 2:
+                ref = xp.at[t, :, hi, ry]
+                out["fwd"].append(send(ref, ref, zfs.at[t, dy], zfr.at[t, dy], dn_dev))
+        for j, block in ((1, lo), (2, hi)):
+            ref = xp.at[t, :, block]
+            out["sib"].append(send(ref, ref, sib_s.at[t, j], sib_r.at[t, j], sib_dev))
+
+    def gather_last(t, out):
+        for copy in out["fwd"]:
+            copy.wait_recv()
+        ref = xp.at[t, :, zo * 2 + c]
+        out["sib"].append(send(ref, ref, sib_s.at[t, 3], sib_r.at[t, 3], sib_dev))
+
+    grad_moe = (gout[...].astype(F32) * 0.5).astype(BF16)
+    pack(grad_moe, 0)
+    pl.semaphore_wait(barrier, len(partners))
+    grad_copies = plane_sends(0)
+
+    source = frames[...].astype(F32)
+    xhat, _ = normalise(source)
+    normed = (xhat * gain_c[...]).astype(BF16)
+    normed_o[...] = normed
+    loads[0].wait()
+    for block in range(2):
+        cols = pl.ds(block * 768, 768)
+        mixed_o[:, cols] = dot_nn(normed, win_v[:, cols])
+    glu = (mixed_o[:, 0:768] * jax.nn.sigmoid(mixed_o[:, 768:1536])).astype(BF16)
+    glu_o[16:144] = glu
+    halo = [
+        send(glu_o.at[128:144], glu_o.at[0:16], halo_s.at[0, 0], halo_r.at[0, 0], next_dev),
+        send(glu_o.at[16:32], glu_o.at[144:160], halo_s.at[0, 1], halo_r.at[0, 1], prev_dev),
+    ]
+    grad_out_state = gather_first(0, grad_copies)
+    for copy in halo:
+        copy.wait_recv()
+
+    @pl.when(seq == 0)
+    def _():
+        glu_o[0:16] = jnp.zeros((16, 768), BF16)
+
+    @pl.when(seq == 7)
+    def _():
+        glu_o[144:160] = jnp.zeros((16, 768), BF16)
+
+    shift_copies(glu_o, shifted)
+    conv_taps(shifted, dw, conv_o, False)
+    conv = conv_o[...]
+    act = (conv * jax.nn.sigmoid(conv)).astype(BF16)
+    act_o[...] = act
+    loads[1].wait()
+    hidden = frames[...].astype(F32) + dot_nn(act, wout_v[...])
+    hidden_o[...] = hidden
+    xhat2, _ = normalise(hidden)
+    pack((xhat2 * gain_m[...]).astype(BF16), 1)
+    moe_copies = plane_sends(1)
+    gather_forward(0, grad_out_state)
+    moe_state = gather_first(1, moe_copies)
+    gather_last(0, grad_out_state)
+    loads[2].wait()
+    loads[3].wait()
+
+    def expert_pair(zz):
+        def one(l, _):
+            rows = pl.ds(pl.multiple_of(zz * 128, 128), 128)
+            g = xp[0, l, pl.ds(2 * zz, 2)].reshape(128, 768)
+            h = xp[1, l, pl.ds(2 * zz, 2)].reshape(128, 768)
+            slope = dot_nt(g, wdn_v[l])
+            pre = dot_nn(h, wup_v[l])
+            s = jax.nn.sigmoid(pre)
+            gp = (slope * (s + pre * s * (1.0 - s))).astype(BF16)
+            ua = (pre * s).astype(BF16)
+            gpre_o[l, rows] = gp
+            up_o[l, rows] = ua
+            y_v[0, l, zz] = dot_nt(gp, wup_v[l]).astype(BF16).reshape(2, 4, 16, 768)
+            y_v[1, l, zz] = dot_nn(ua, wdn_v[l]).astype(BF16).reshape(2, 4, 16, 768)
+            return 0
+
+        lax.fori_loop(0, 4, one, 0)
+
+    csib = {}
+
+    def return_pair(j, zz):
+        for t in range(2):
+            csib[t, j] = send(
+                y_v.at[t, :, zz, 1 - c], sr.at[t, :, zz], csib_s.at[t, j], csib_r.at[t, j], sib_dev
+            )
+
+    gather_forward(1, moe_state)
+    grad_out_state["sib"][0].wait_recv()
+    moe_state["sib"][0].wait_recv()
+    expert_pair(z)
+    return_pair(0, z)
+    gather_last(1, moe_state)
+    for j, zz in ((1, zd), (2, zu), (3, zo)):
+        grad_out_state["sib"][j].wait_recv()
+        moe_state["sib"][j].wait_recv()
+        expert_pair(zz)
+        return_pair(j, zz)
+
+    def add_into(t, zz, other, lo, hi):
+        for l in range(4):
+            a = sr[t, l, zz, lo:hi].astype(F32)
+            sr[t, l, zz, lo:hi] = (a + other(l).astype(F32)).astype(BF16)
+
+    def sibling_sum(t, j, zz):
+        csib[t, j].wait_recv()
+        add_into(t, zz, lambda l: y_v[t, l, zz, c], 0, 4)
+
+    a256 = iota((256, 256), 0)
+    unperm = (
+        ((a256 // 4) % 4) * 64 + (a256 // 64) * 16 + ((a256 // 16) % 4) * 4 + a256 % 4
+        == iota((256, 256), 1)
+    ).astype(F32).astype(BF16)
+
+    def collect_z(t):
+        sibling_sum(t, 3, zo)
+        f_up = send(sr.at[t, :, zo, 0:2], ruf.at[t], cz_s.at[t, 0], cz_r.at[t, 0], up_dev)
+        f_dn = send(sr.at[t, :, zo, 2:4], rdf.at[t], cz_s.at[t, 1], cz_r.at[t, 1], dn_dev)
+        sibling_sum(t, 2, zu)
+        u_hi = send(sr.at[t, :, zu, 2:4], ru.at[t, :, 2:4], cz_s.at[t, 2], cz_r.at[t, 2], up_dev)
+        sibling_sum(t, 1, zd)
+        d_lo = send(sr.at[t, :, zd, 0:2], rd.at[t, :, 0:2], cz_s.at[t, 3], cz_r.at[t, 3], dn_dev)
+        sibling_sum(t, 0, z)
+        return [f_up, f_dn, u_hi, d_lo]
+
+    def collect_forward(t, state):
+        state[0].wait_recv()
+        add_into(t, zu, lambda l: ruf[t, l], 0, 2)
+        state.append(send(sr.at[t, :, zu, 0:2], ru.at[t, :, 0:2], cz_s.at[t, 4], cz_r.at[t, 4], up_dev))
+        state[1].wait_recv()
+        add_into(t, zd, lambda l: rdf[t, l], 2, 4)
+        state.append(send(sr.at[t, :, zd, 2:4], rd.at[t, :, 2:4], cz_s.at[t, 5], cz_r.at[t, 5], dn_dev))
+
+    def collect_plane(t, state):
+        for copy in state[2:]:
+            copy.wait_recv()
+        parts = []
+        for l in range(4):
+            total = sr[t, l, z].astype(F32) + ru[t, l].astype(F32) + rd[t, l].astype(F32)
+            parts.append(total.astype(BF16).reshape(64, 768))
+        total = jnp.concatenate(parts, axis=0)
+        fs[t] = dot_nn(unperm, total).astype(BF16).reshape(4, 4, 16, 768)
+        own = pltpu.make_async_copy(fs.at[t, y, x], gr.at[t, y, x], loc_sem.at[2 + t])
+        own.start()
+        copies = [own]
+        for i, (dy, dx) in enumerate(offsets):
+            if i == 0:
+                continue
+            ty, tx = plane_to(dy, dx)
+            copies.append(
+                send(fs.at[t, ty, tx], gr.at[t, y, x], cp_s.at[t, i], cp_r.at[t, i],
+                     (seq, ty * 4 + tx))
+            )
+        return copies
+
+    def collect_last(t, copies):
+        copies[0].wait()
+        for copy in copies[1:]:
+            copy.wait_recv()
+        return dot_tn(pt[...], gr[t].reshape(256, 768))
+
+    back = collect_z(0)
+    out = collect_z(1)
+    collect_forward(0, back)
+    collect_forward(1, out)
+    back_copies = collect_plane(0, back)
+    gmi_o[...] = collect_last(0, back_copies)
+    out_copies = collect_plane(1, out)
+    eo_o[...] = collect_last(1, out_copies)
+    for l in range(4):
+        rows_o[l] = xp[1, l].reshape(512, 768)
+        grows_o[l] = xp[0, l].reshape(512, 768)
+    for copy in sent:
+        copy.wait_send()
+
+
+def run_fused(*operands):
+    any_spec = pl.BlockSpec(memory_space=pl.ANY)
+    vmem = pl.BlockSpec(memory_space=pltpu.VMEM)
+    dma = pltpu.SemaphoreType.DMA
+    return pl.pallas_call(
+        fused_kernel,
+        out_shape=[
+            jax.ShapeDtypeStruct(shape, dtype)
+            for shape, dtype in (
+                ((128, 768), F32), ((128, 768), F32), ((128, 768), F32), ((128, 768), F32),
+                ((160, 768), BF16), ((128, 1536), F32), ((128, 768), BF16), ((128, 768), BF16),
+                ((4, 512, 768), BF16), ((4, 512, 768), BF16),
+                ((4, 512, 384), BF16), ((4, 512, 384), BF16),
+            )
+        ],
+        in_specs=[vmem, vmem, any_spec, vmem, any_spec, vmem, any_spec, any_spec, vmem, vmem, vmem],
+        out_specs=[vmem] * 12,
+        scratch_shapes=[
+            pltpu.VMEM((768, 1536), BF16),
+            pltpu.VMEM((768, 768), BF16),
+            pltpu.VMEM((4, 768, 384), BF16),
+            pltpu.VMEM((4, 384, 768), BF16),
+            dma((4,)),
+            pltpu.VMEM((256, 128), BF16),
+            pltpu.VMEM((2, 4, 4, 16, 768), BF16),
+            pltpu.VMEM((2, 4, 4, 16, 768), BF16),
+            pltpu.VMEM((2, 4, 8, 4, 16, 768), BF16),
+            pltpu.VMEM((8, 160, 768), F32),
+            pltpu.VMEM((2, 4, 4, 2, 4, 16, 768), BF16),
+            pltpu.VMEM((2, 4, 4, 4, 16, 768), BF16),
+            pltpu.VMEM((2, 4, 2, 16, 768), BF16),
+            pltpu.VMEM((2, 4, 2, 16, 768), BF16),
+            pltpu.VMEM((2, 4, 4, 16, 768), BF16),
+            pltpu.VMEM((2, 4, 4, 16, 768), BF16),
+            pltpu.VMEM((2, 4, 4, 16, 768), BF16),
+            pltpu.VMEM((2, 4, 4, 16, 768), BF16),
+            dma((2, 16)), dma((2, 16)), dma((1, 2)), dma((1, 2)),
+            dma((2, 2, 4)), dma((2, 2, 4)), dma((2, 4)), dma((2, 4)), dma((2, 4)), dma((2, 4)),
+            dma((2, 4)), dma((2, 4)), dma((2, 6)), dma((2, 6)), dma((2, 16)), dma((2, 16)), dma((4,)),
+        ],
+        compiler_params=pltpu.CompilerParams(
+            collective_id=0, has_side_effects=True, vmem_limit_bytes=62 * 1024 * 1024
+        ),
+    )(*operands)
 
 
 def per_device(
@@ -87,57 +447,22 @@
     dense_scale = (length * seq_count * exp_count) ** (-0.5)
     expert_scale = (seq_count * exp_count * capacity) ** (-0.5)
     source = frames_in[0].astype(jnp.float32)
-    normed = layer_norm(source, gain_conv).astype(jnp.bfloat16)
-    mixed_cols = jnp.dot(normed, w_in, preferred_element_type=jnp.float32)
-    glu_out = gated_linear(mixed_cols).astype(jnp.bfloat16)
-    glu_pad = extended(glu_out, (("seq", 0),), half_kernel)
-    conv_out = depthwise(glu_pad, dw_kernel, length)
-    act_out = swish_act(conv_out).astype(jnp.bfloat16)
-    hidden = source + jnp.dot(act_out, w_out, preferred_element_type=jnp.float32)
-    moe_in = layer_norm(hidden, gain_moe).astype(jnp.bfloat16)
-    column = route[0] * capacity + slot[0]
-    slot_table = (column[:, None] == jnp.arange(slot_count, dtype=jnp.int32)[None, :]).astype(
-        jnp.bfloat16
-    )
-
-    def pack_slots(values):
-        packed = jnp.einsum(
-            "ls,ld->sd", slot_table, values, preferred_element_type=jnp.float32
-        ).astype(jnp.bfloat16)
-        return packed.reshape(exp_count, slot_count // exp_count, feat_width)
-
-    def unpack_slots(values):
-        return jnp.dot(
-            slot_table, values.reshape(slot_count, feat_width), preferred_element_type=jnp.float32
-        )
-
-    expert_rows = spread(pack_slots(moe_in), seq_count)
-    senders = expert_rows.shape[0]
-    expert_rows = expert_rows.reshape(senders, local_experts, capacity, feat_width)
-    pre_act = jnp.einsum("recd,edf->recf", expert_rows, w_up, preferred_element_type=jnp.float32)
-    up_act = swish_act(pre_act).astype(jnp.bfloat16)
-    partial_value = jnp.einsum("recf,efd->recd", up_act, w_down, preferred_element_type=jnp.float32)
-    expert_out = unpack_slots(
-        collect(partial_value.reshape(senders, local_experts * capacity, feat_width), seq_count)
-    )
+    (
+        expert_out, grad_moe_in, hidden, conv_out, glu_rows, mixed_cols, normed, act_out,
+        expert_rows, grad_rows, up_act, grad_pre,
+    ) = run_fused(
+        frames_in[0], gain_conv[None], w_in, dw_kernel, w_out, gain_moe[None], w_up, w_down,
+        route, slot, grad_out[0],
+    )
+    glu_pad = glu_rows[1:159]
     block_out = (hidden + 0.5 * expert_out).astype(jnp.bfloat16)
-    grad_moe = (0.5 * grad_out[0].astype(jnp.float32)).astype(jnp.bfloat16)
-    grad_rows = spread(pack_slots(grad_moe), seq_count).reshape(
-        senders, local_experts, capacity, feat_width
-    )
-    slope_back = jnp.einsum("recd,efd->recf", grad_rows, w_down, preferred_element_type=jnp.float32)
-    grad_pre = (slope_back * swish_slope(pre_act)).astype(jnp.bfloat16)
     grad_w_down = (
-        jnp.einsum("recf,recd->efd", up_act, grad_rows, preferred_element_type=jnp.float32)
+        jnp.einsum("erf,erd->efd", up_act, grad_rows, preferred_element_type=jnp.float32)
         * expert_scale
     )
     grad_w_up = (
-        jnp.einsum("recd,recf->edf", expert_rows, grad_pre, preferred_element_type=jnp.float32)
+        jnp.einsum("erd,erf->edf", expert_rows, grad_pre, preferred_element_type=jnp.float32)
         * expert_scale
-    )
-    back_part = jnp.einsum("recf,edf->recd", grad_pre, w_up, preferred_element_type=jnp.float32)
-    grad_moe_in = unpack_slots(
-        collect(back_part.reshape(senders, local_experts * capacity, feat_width), seq_count)
     )
     _, pull_back = jax.vjp(layer_norm, hidden, gain_moe)
     back_hidden, gain_moe_term = pull_back(grad_moe_in)

time: 328 us -> 215 us (0.66)
  Pallas kernels: 0 us -> 98.6 us
  waiting for transfers between devices: 127 us -> 35.3 us
  local copies, waits for them, and re-layouts: 79.4 us -> 32 us
  starting transfers between devices: 50.1 us -> 12 us
  matrix products: 36.4 us -> 16.7 us
  other arithmetic: 31.2 us -> 18 us
    pallas_call x0 -> x1, Pallas kernels: none -> 98.6 us  [run_fused(): pl.pallas_call(fused_kernel, out_shape=[jax.ShapeDtypeStruct(shape, dtype...]
    all_to_all x4 -> x0, waiting for transfers between devices: 86.1 us -> none  [the longest x2 53.1 us: spread(): lax.all_to_all(copies, ('seq', 'exp'), split_axis=0, concat_axis=0, tiled...]
    all_to_all x4 -> x0, starting transfers between devices: 28.5 us -> none  [the longest x2 19 us: spread(): lax.all_to_all(copies, ('seq', 'exp'), split_axis=0, concat_axis=0, tiled...]
    another operation x32, local copies, waits for them, and re-layouts: 23.8 us -> 0.32 us  [tap_sums(): return jnp.stack(tap_rows)]
    dot_general x12 -> x2, matrix products: 27.9 us -> 9.75 us  [the longest x1 6.07 us: per_device(): jnp.einsum('erd,erf->edf', expert_rows, grad_pre, preferred_element_type=...]
    ppermute x2 -> x1, waiting for transfers between devices: 10.6 us -> 0.01 us  [extended(): after = lax.ppermute(initial, axis, down)]
    all_to_all x2 -> x0, local copies, waits for them, and re-layouts: 7.51 us -> none  [spread(): lax.all_to_all(copies, ('seq', 'exp'), split_axis=0, concat_axis=0, tiled...]
    unnamed x164 -> x48, local copies, waits for them, and re-layouts: 13.4 us -> 6.2 us
  transfers between devices with their start and end apart: 9 -> 3, of which waited for: 5 -> 1; matrix products, arithmetic and copies ran while one was open for 35% -> 11% of each run, Pallas kernels for 0% -> 0%
where the time goes in v2:
time: 215 us; the launch traced here: 214 us
  Pallas kernels  98.6 us (46%)
  waiting for transfers between devices  35.3 us (16%)
  local copies, waits for them, and re-layouts  32 us (15%)
  other arithmetic  18 us (8%)
  matrix products  16.7 us (8%)
  starting transfers between devices  12 us (6%)
    pallas_call x1, Pallas kernels, run_fused(): pl.pallas_call(fused_kernel, out_shape=[jax.ShapeDtypeStruct(shape, dtype...  98.6 us
    all_to_all x1, waiting for transfers between devices, per_device(): lax.all_to_all(sent, ('seq', 'exp'), split_axis=0, concat_axis=0, tiled=T...  35.3 us
    reshape x3, local copies, waits for them, and re-layouts, by_rows(): return value.reshape(devices, -1)  8.17 us
    all_to_all x1, starting transfers between devices, per_device(): lax.all_to_all(sent, ('seq', 'exp'), split_axis=0, concat_axis=0, tiled=T...  6.94 us
    unnamed x48, local copies, waits for them, and re-layouts  6.2 us
    dot_general x1, matrix products, per_device(): jnp.einsum('erd,erf->edf', expert_rows, grad_pre, preferred_element_type=...  6.07 us
    concatenate x1, local copies, waits for them, and re-layouts, per_device(): jnp.concatenate([by_rows(grad_w_in), by_rows(grad_w_out), by_rows(grad_dw...  5.96 us
  transfers between devices with their start and end apart: 3, of which 1 were waited for; matrix products, arithmetic and copies ran while one was open for 11% of the time, Pallas kernels for 0%

profile of v2, /device:TPU:1, one launch (start us, length us, event | category | flops | bytes accessed | tf_op | source)
XLA Modules:
  0.0 213.8 jit_solution(15471864045827821592)
XLA Ops:
  0.6 1.3 broadcast_in_dim.31.gain_m
  1.9 1.3 broadcast_in_dim.30.gain_c
  3.2 98.6 %shard_map.178 = (f32[128,768]{1,0:T(8,128)}, f32[128,768]{1,0:T(8,128)}, f32[128,768]{1,0:T(8,128)}, f32[128,768]{1,0:T(8,128)}, bf16[160,768]{1,0:T(8,128)(2,1...) custom-call(bf16[128,768]{1,0:T(8,128)(2,1)} %bitcast.35, ...), custom_call_target="tpu_custom_call" | custom-call | tf_op jit(solution)/shard_map/pallas_call | solution.py:393
  101.8 1.2 reduce_sum.402
  104.3 1.4 multiply_reduce_fusion
  105.7 2.1 fusion.97
  110.1 1.9 collective-permute-start
  112.0 3.2 %collective-permute-start.1 = (bf16[15,768]{1,0:T(8,128)(2,1)}, bf16[15,768]{1,0:T(8,128)(2,1)}, u32[]{:S(2)}, u32[]{:S(2)}) collective-permute-start(bf16[15,768]{1,0:T(8,128)(2,1)} %get-tuple-element.107), channel_id=1, source_target_pairs={{16,0},{32,16},{48,32},{64,48},{80,64},{96,80},{112,96},{17,1},{33... | collective-permute-start | bytes 69128 | tf_op jit(solution)/shard_map/ppermute | solution.py:19
  119.2 1.5 multiply_convert_fusion.1
  120.7 1.8 slice_reduce_fusion.29
  122.5 1.4 mul.732
  125.7 3.0 %reshape.116 = bf16[128,4608]{1,0:T(8,128)(2,1)} reshape(bf16[768,768]{1,0:T(8,128)(2,1)} %multiply_convert_fusion.1) | data formatting | bytes 2359296 | tf_op jit(solution)/shard_map/reshape | solution.py:495
  128.7 4.3 %fusion.9 = (f32[128,768]{1,0:T(8,128)S(1)}, f32[128,768]{1,0:T(8,128)S(1)}) fusion(f32[128,1536]{1,0:T(8,128)} %get-tuple-element.24, bf16[15,768]{1,0:T(8,128)(2,1)} %collective-permute-done.1, bf16[128,768]{1,0:T(8,128)(2,1)S(1)} %get-tuple-element.113, f32[768]{0:T(1024)} %get-tuple-element.99, f32[768]{0:T(1024)} %get-tuple-element.100, ...), kind=kLoop, calls=%fused_computation.82 | loop fusion | flops 18579456 | bytes 1910784 | tf_op jit(solution)/shard_map/transpose(jvp())/mul | solution.py:41
  133.0 1.3 fusion.88
  137.1 3.3 %multiply_convert_fusion = bf16[768,1536]{1,0:T(8,128)(2,1)} fusion(bf16[128,768]{1,0:T(8,128)(2,1)} %get-tuple-element.26, f32[128,768]{1,0:T(8,128)S(1)} %fusion.88, f32[128,768]{1,0:T(8,128)} %copy-done.7), kind=kOutput, calls=%fused_computation.1 | convolution fusion | flops 304742400 | bytes 3342336 | tf_op jit(solution)/shard_map/ld,le->de/dot_general | solution.py:485
  140.4 4.4 %reshape.115 = bf16[128,9216]{1,0:T(8,128)(2,1)S(1)} reshape(bf16[768,1536]{1,0:T(8,128)(2,1)} %multiply_convert_fusion) | data formatting | bytes 4718592 | tf_op jit(solution)/shard_map/reshape | solution.py:495
  144.8 6.0 %concatenate.41 = bf16[128,14022]{1,0:T(8,128)(2,1)} concatenate(bf16[128,9216]{1,0:T(8,128)(2,1)S(1)} %reshape.115, bf16[128,4608]{1,0:T(8,128)(2,1)} %reshape.116, bf16[128,186]{1,0:T(8,128)(2,1)S(1)} %copy-done.12, bf16[128,6]{1,0:T(8,128)(2,1)S(1)} %copy-done.15, bf16[128,6]{1,0:T(8,128)(2,1)S(1)} %copy-done.14), dimensions={1} | concatenate | bytes 7179264 | tf_op jit(solution)/shard_map/concatenate | solution.py:497
  150.7 2.4 %pad_bitcast_fusion = bf16[16,8,112,128]{3,1,2,0:T(8,128)(2,1)S(1)} fusion(bf16[128,14022]{1,0:T(8,128)(2,1)} %concatenate.41), kind=kLoop, calls=%fused_computation.2 | loop fusion | bytes 7259648
  153.1 2.6 %copy.27 = bf16[16,8,112,128]{3,2,1,0:T(8,128)(2,1)} copy(bf16[16,8,112,128]{3,1,2,0:T(8,128)(2,1)S(1)} %pad_bitcast_fusion) | data formatting | bytes 7340032
  155.7 6.9 %all-to-all-start = ((bf16[128,112,128]{2,1,0:T(8,128)(2,1)}), bf16[128,112,128]{2,1,0:T(8,128)(2,1)}, u32[]{:S(2)}, u32[]{:S(2)}) async-start(bf16[128,112,128]{2,1,0:T(8,128)(2,1)} %bitcast.34), calls=%async_computation | async-start | bytes 7340032 | tf_op jit(solution)/shard_map/all_to_all | solution.py:510
  162.7 6.1 %broadcast_multiply_fusion.1 = f32[4,768,384]{2,1,0:T(8,128)} fusion(bf16[4,512,768]{2,1,0:T(8,128)(2,1)} %get-tuple-element.29, bf16[4,512,384]{2,1,0:T(8,128)(2,1)S(1)} %copy-done.9), kind=kOutput, calls=%fused_computation.36 | convolution fusion | flops 1209139200 | bytes 9437184 | tf_op jit(solution)/shard_map/erd,erf->edf/dot_general | solution.py:464
  168.8 3.7 %broadcast_multiply_fusion = f32[4,384,768]{2,1,0:T(8,128)} fusion(bf16[4,512,384]{2,1,0:T(8,128)(2,1)S(1)} %copy-done.4, bf16[4,512,768]{2,1,0:T(8,128)(2,1)S(1)} %copy-done.2), kind=kOutput, calls=%fused_computation.35 | convolution fusion | flops 1209139200 | bytes 9437184 | tf_op jit(solution)/shard_map/erf,erd->efd/dot_general | solution.py:460
  173.4 35.3 %all-to-all-done = bf16[128,112,128]{2,1,0:T(8,128)(2,1)} async-done(((bf16[128,112,128]{2,1,0:T(8,128)(2,1)}), bf16[128,112,128]{2,1,0:T(8,128)(2,1)}, u32[]{:S(2)}, u32[]{:S(2)}) %all-to-all-start) | async-done | bytes 3670048 | tf_op jit(solution)/shard_map/all_to_all | solution.py:510
  208.7 2.6 %convert_reduce_fusion = f32[112,128]{1,0:T(8,128)S(1)} fusion(bf16[128,112,128]{2,1,0:T(8,128)(2,1)} %all-to-all-done), kind=kLoop, calls=%fused_computation | loop fusion | flops 3655680 | bytes 3727360 | tf_op jit(solution)/shard_map/reduce_sum | solution.py:511
  (110 shorter events, 15.3 us)
Async XLA Ops:
  3.2 101.1 %copy-start.17 = (f32[768]{0:T(1024)S(1)}, f32[768]{0:T(1024)}, u32[]{:S(2)}) copy-start(f32[768]{0:T(1024)} %param.16) | copy-start | bytes 9220
  101.8 6.0 %copy-start.8 = (bf16[1,128,768]{2,1,0:T(8,128)(2,1)S(1)}, bf16[1,128,768]{2,1,0:T(8,128)(2,1)}, u32[]{:S(2)}) copy-start(bf16[1,128,768]{2,1,0:T(8,128)(2,1)} %param.21) | copy-start | bytes 589828
  101.8 6.5 %copy-start = (bf16[160,768]{1,0:T(8,128)(2,1)S(1)}, bf16[160,768]{1,0:T(8,128)(2,1)}, u32[]{:S(2)}) copy-start(bf16[160,768]{1,0:T(8,128)(2,1)} %get-tuple-element.28) | copy-start | bytes 737284
  101.8 6.5 %copy-start.10 = (bf16[768,768]{1,0:T(8,128)(2,1)S(1)}, bf16[768,768]{1,0:T(8,128)(2,1)}, u32[]{:S(2)}) copy-start(bf16[768,768]{1,0:T(8,128)(2,1)} %w_out.1) | copy-start | bytes 3538948
  101.8 6.4 %copy-start.22 = (f32[128,768]{1,0:T(8,128)S(1)}, f32[128,768]{1,0:T(8,128)}, u32[]{:S(2)}) copy-start(f32[128,768]{1,0:T(8,128)} %get-tuple-element.25) | copy-start | bytes 1179652
  108.3 6.9 %copy-start.3 = (bf16[1,128,768]{2,1,0:T(8,128)(2,1)S(1)}, bf16[1,128,768]{2,1,0:T(8,128)(2,1)}, u32[]{:S(2)}) copy-start(bf16[1,128,768]{2,1,0:T(8,128)(2,1)} %param.11) | copy-start | bytes 589828
  108.3 7.1 %copy-start.11 = (f32[31,768]{1,0:T(8,128)S(1)}, f32[31,768]{1,0:T(8,128)}, u32[]{:S(2)}) copy-start(f32[31,768]{1,0:T(8,128)} %dw.1) | copy-start | bytes 285700
  109.5 9.7 %copy-start.13 = (bf16[128,768]{1,0:T(8,128)(2,1)S(1)}, bf16[128,768]{1,0:T(8,128)(2,1)}, u32[]{:S(2)}) copy-start(bf16[128,768]{1,0:T(8,128)(2,1)} %get-tuple-element.27) | copy-start | bytes 589828
  110.1 18.6 %collective-permute-start = (bf16[15,768]{1,0:T(8,128)(2,1)}, bf16[15,768]{1,0:T(8,128)(2,1)}, u32[]{:S(2)}, u32[]{:S(2)}) collective-permute-start(bf16[15,768]{1,0:T(8,128)(2,1)} %get-tuple-element.106), channel_id=1, source_target_pairs={{0,16},{16,32},{32,48},{48,64},{64,80},{80,96},{96,112},{1,17},{17... | collective-permute-start | bytes 69128 | tf_op jit(solution)/shard_map/ppermute | solution.py:18
  112.0 16.6 %collective-permute-start.1 = (bf16[15,768]{1,0:T(8,128)(2,1)}, bf16[15,768]{1,0:T(8,128)(2,1)}, u32[]{:S(2)}, u32[]{:S(2)}) collective-permute-start(bf16[15,768]{1,0:T(8,128)(2,1)} %get-tuple-element.107), channel_id=1, source_target_pairs={{16,0},{32,16},{48,32},{64,48},{80,64},{96,80},{112,96},{17,1},{33... | collective-permute-start | bytes 69128 | tf_op jit(solution)/shard_map/ppermute | solution.py:19
  120.7 13.5 %copy-start.1 = (bf16[768,1536]{1,0:T(8,128)(2,1)S(1)}, bf16[768,1536]{1,0:T(8,128)(2,1)}, u32[]{:S(2)}) copy-start(bf16[768,1536]{1,0:T(8,128)(2,1)} %w_in.1) | copy-start | bytes 7077892
  120.7 13.6 %copy-start.16 = (f32[768]{0:T(1024)S(1)}, f32[768]{0:T(1024)}, u32[]{:S(2)}) copy-start(f32[768]{0:T(1024)} %param.12) | copy-start | bytes 9220
  128.7 5.6 %copy-start.18 = (f32[128]{0:T(128)S(1)}, f32[128]{0:T(128)}, u32[]{:S(2)}) copy-start(f32[128]{0:T(128)} %broadcast_multiply_fusion.2) | copy-start | bytes 1540
  133.0 3.3 %copy-start.7 = (f32[128,768]{1,0:T(8,128)}, f32[128,768]{1,0:T(8,128)S(1)}, u32[]{:S(2)}) copy-start(f32[128,768]{1,0:T(8,128)S(1)} %get-tuple-element.101) | copy-start | bytes 1179652
  140.4 4.4 %copy-start.12 = (bf16[128,186]{1,0:T(8,128)(2,1)S(1)}, bf16[128,186]{1,0:T(8,128)(2,1)}, u32[]{:S(2)}) copy-start(bf16[128,186]{1,0:T(8,128)(2,1)} %reshape.117) | copy-start | bytes 142852
  140.4 4.4 %copy-start.14 = (bf16[128,6]{1,0:T(8,128)(2,1)S(1)}, bf16[128,6]{1,0:T(8,128)(2,1)}, u32[]{:S(2)}) copy-start(bf16[128,6]{1,0:T(8,128)(2,1)} %mul.732) | copy-start | bytes 4612
  140.4 4.4 %copy-start.15 = (bf16[128,6]{1,0:T(8,128)(2,1)S(1)}, bf16[128,6]{1,0:T(8,128)(2,1)}, u32[]{:S(2)}) copy-start(bf16[128,6]{1,0:T(8,128)(2,1)} %mul.728) | copy-start | bytes 4612
  155.7 7.0 %copy-start.9 = (bf16[4,512,384]{2,1,0:T(8,128)(2,1)S(1)}, bf16[4,512,384]{2,1,0:T(8,128)(2,1)}, u32[]{:S(2)}) copy-start(bf16[4,512,384]{2,1,0:T(8,128)(2,1)} %get-tuple-element.30) | copy-start | bytes 4718596
  155.7 52.9 %all-to-all-start = ((bf16[128,112,128]{2,1,0:T(8,128)(2,1)}), bf16[128,112,128]{2,1,0:T(8,128)(2,1)}, u32[]{:S(2)}, u32[]{:S(2)}) async-start(bf16[128,112,128]{2,1,0:T(8,128)(2,1)} %bitcast.34), calls=%async_computation | async-start | bytes 7340032 | tf_op jit(solution)/shard_map/all_to_all | solution.py:510
  162.7 6.1 %copy-start.2 = (bf16[4,512,768]{2,1,0:T(8,128)(2,1)S(1)}, bf16[4,512,768]{2,1,0:T(8,128)(2,1)}, u32[]{:S(2)}) copy-start(bf16[4,512,768]{2,1,0:T(8,128)(2,1)} %get-tuple-element.32) | copy-start | bytes 9437188
  162.7 6.1 %copy-start.4 = (bf16[4,512,384]{2,1,0:T(8,128)(2,1)S(1)}, bf16[4,512,384]{2,1,0:T(8,128)(2,1)}, u32[]{:S(2)}) copy-start(bf16[4,512,384]{2,1,0:T(8,128)(2,1)} %get-tuple-element.31) | copy-start | bytes 4718596
  168.8 3.7 %copy-start.6 = (f32[128,768]{1,0:T(8,128)S(1)}, f32[128,768]{1,0:T(8,128)}, u32[]{:S(2)}) copy-start(f32[128,768]{1,0:T(8,128)} %copy-done.5) | copy-start | bytes 1179652
  168.8 3.7 %copy-start.19 = (f32[128]{0:T(128)S(1)}, f32[128]{0:T(128)}, u32[]{:S(2)}) copy-start(f32[128]{0:T(128)} %broadcast_multiply_fusion.2) | copy-start | bytes 1540
  168.8 3.7 %copy-start.21 = (f32[128]{0:T(128)S(1)}, f32[128]{0:T(128)}, u32[]{:S(2)}) copy-start(f32[128]{0:T(128)} %copy-done.20) | copy-start | bytes 1540
  (2 other events, 1.3 us)

commit v3 on v2

--- a/solution.py
+++ b/solution.py
@@ -6,61 +6,6 @@
 from jax.sharding import PartitionSpec as P
 
 NORM_EPSILON = 1e-05
-
-
-def extended(shard, sides, width):
-    for axis, dim in sides:
-        size, length = (lax.axis_size(axis), shard.shape[dim])
-        up = [(i, (i + 1) % size) for i in range(size - 1)]
-        down = [(j, i) for i, j in up]
-        last = lax.slice_in_dim(shard, length - width, length, axis=dim)
-        initial = lax.slice_in_dim(shard, 0, width, axis=dim)
-        before = lax.ppermute(last, axis, up)
-        after = lax.ppermute(initial, axis, down)
-        shard = jnp.concatenate([before, shard, after], axis=dim)
-    return shard
-
-
-def layer_norm(frame_rows, gain_vec):
-    centre = frame_rows - jnp.mean(frame_rows, axis=-1, keepdims=True)
-    spread = jnp.mean(centre * centre, axis=-1, keepdims=True)
-    return centre * lax.rsqrt(spread + NORM_EPSILON) * gain_vec
-
-
-def swish_act(values):
-    return values * jax.nn.sigmoid(values)
-
-
-def swish_slope(values):
-    logistic = jax.nn.sigmoid(values)
-    return logistic + values * logistic * (1.0 - logistic)
-
-
-def gated_linear(mixed_cols):
-    feat_width = mixed_cols.shape[-1] // 2
-    return mixed_cols[..., :feat_width] * jax.nn.sigmoid(mixed_cols[..., feat_width:])
-
-
-def depthwise(padded, kernel, length):
-    summed_taps = jnp.zeros(padded.shape[:-2] + (length, padded.shape[-1]), jnp.float32)
-    for tap_index in range(kernel.shape[0]):
-        summed_taps = summed_taps + kernel[tap_index] * padded[
-            ..., tap_index : tap_index + length, :
-        ].astype(jnp.float32)
-    return summed_taps
-
-
-def tap_sums(padded, grad_conv, length, tap_count):
-    reduce_axes = tuple(range(grad_conv.ndim - 1))
-    tap_rows = []
-    for tap_index in range(tap_count):
-        window = padded[..., tap_index : tap_index + length, :].astype(jnp.float32)
-        tap_rows.append(jnp.sum(grad_conv * window, axis=reduce_axes))
-    return jnp.stack(tap_rows)
-
-
-NZ = 4
-NX = 4
 BF16 = jnp.bfloat16
 F32 = jnp.float32
 MESH = pl.DeviceIdType.MESH
@@ -93,6 +38,16 @@
     shifted[0] = padded[...].astype(F32)
     for s in range(1, 8):
         shifted[s, 0:152] = shifted[0, s : s + 152]
+
+
+def tap_grads(shifted, grads, out):
+    for block in range(6):
+        cols = pl.ds(block * 128, 128)
+        own = grads[16:144, cols].astype(F32)
+        for k in range(31):
+            a, s = divmod(k + 1, 8)
+            term = own * shifted[s, 8 * a : 8 * a + 128, cols]
+            out(k, cols, jnp.sum(term, axis=0, keepdims=True))
 
 
 def conv_taps(shifted, dw, out, flip):
@@ -108,12 +63,18 @@
 
 def fused_kernel(
     frames, gain_c, w_in, dw, w_out, gain_m, w_up, w_down, route, slot, gout,
-    eo_o, gmi_o, hidden_o, conv_o, glu_o, mixed_o, normed_o, act_o, rows_o, grows_o, up_o, gpre_o,
+    block_o, gx_o, gwi_o, gwo_o, ext_o, ewu_o, ewd_o,
     win_v, wout_v, wup_v, wdn_v, load_sem,
     pt, pk, raw, xp, shifted, y_v, sr, ruf, rdf, ru, rd, fs, gr,
+    hidden_o, conv_o, glu_o, mixed_o, normed_o, act_o, up_o, gpre_o,
+    ewu_v, ewd_v, gc_pad, shifted_b, ap, aps, hbx, gmx, terms_v, gg_v,
+    sa, ra, sb, rb, td, sd, rdd, sax, rax, sbx, rbx, tdx, sdx, rdx,
     pl_s, pl_r, halo_s, halo_r, zs, zr, zfs, zfr, sib_s, sib_r,
     csib_s, csib_r, cz_s, cz_r, cp_s, cp_r, loc_sem,
+    xs, xr, ra_s, ra_r, rb_s, rb_r, rd_s, rd_r, store_sem,
 ):
+    dense_scale = 16384**-0.5
+    expert_scale = 512**-0.5
     seq = lax.axis_index("seq")
     exp = lax.axis_index("exp")
     z, c = lax.div(seq, 2), lax.rem(seq, 2)
@@ -136,7 +97,7 @@
         load.start()
 
     barrier = pltpu.get_barrier_semaphore()
-    partners = [up_dev, dn_dev, next_dev, prev_dev]
+    partners = [up_dev, dn_dev, next_dev, prev_dev, (zo * 2 + c, exp)]
     for dy, dx in offsets[1:]:
         ty, tx = plane_to(dy, dx)
         partners.append((seq, ty * 4 + tx))
@@ -223,6 +184,23 @@
         ref = xp.at[t, :, zo * 2 + c]
         out["sib"].append(send(ref, ref, sib_s.at[t, 3], sib_r.at[t, 3], sib_dev))
 
+    def row_choice(part, half):
+        r = iota((384, 1), 0)
+        a = lax.shift_right_logical(r * 683, 16)
+        r = r - a * 96
+        b = lax.shift_right_logical(r * 2731, 16)
+        r = r - b * 24
+        d = lax.shift_right_logical(r * 10923, 16)
+        j = r - d * 6
+        zz, yy, xx = ((a, b, d), (d, a, b), (b, d, a))[part]
+        feature = (((zz * 2 + half) * 4 + yy) * 4 + xx) * 6 + j
+        return (feature == iota((384, 768), 1)).astype(F32).astype(BF16)
+
+    def choose_rows(part, values):
+        ap[part, c] = dot_nt(values, row_choice(part, c)).astype(BF16)
+        aps[part] = dot_nt(values, row_choice(part, 1 - c)).astype(BF16)
+        return send(aps.at[part], ap.at[part, c], xs.at[part], xr.at[part], sib_dev)
+
     grad_moe = (gout[...].astype(F32) * 0.5).astype(BF16)
     pack(grad_moe, 0)
     pl.semaphore_wait(barrier, len(partners))
@@ -230,7 +208,7 @@
 
     source = frames[...].astype(F32)
     xhat, _ = normalise(source)
-    normed = (xhat * gain_c[...]).astype(BF16)
+    normed = (xhat * gain_c[...].reshape(1, 768)).astype(BF16)
     normed_o[...] = normed
     loads[0].wait()
     for block in range(2):
@@ -263,8 +241,9 @@
     hidden = frames[...].astype(F32) + dot_nn(act, wout_v[...])
     hidden_o[...] = hidden
     xhat2, _ = normalise(hidden)
-    pack((xhat2 * gain_m[...]).astype(BF16), 1)
+    pack((xhat2 * gain_m[...].reshape(1, 768)).astype(BF16), 1)
     moe_copies = plane_sends(1)
+    chosen = [choose_rows(part, (normed_o, normed_o, act_o)[part][...]) for part in range(3)]
     gather_forward(0, grad_out_state)
     moe_state = gather_first(1, moe_copies)
     gather_last(0, grad_out_state)
@@ -371,17 +350,173 @@
             copy.wait_recv()
         return dot_tn(pt[...], gr[t].reshape(256, 768))
 
+    def expert_grads():
+        def one(l, _):
+            rows = xp[1, l].reshape(512, 768)
+            ewu_v[l] = (dot_tn(rows, gpre_o[l]) * expert_scale).astype(BF16)
+            grads = xp[0, l].reshape(512, 768)
+            ewd_v[l] = (dot_tn(up_o[l], grads) * expert_scale).astype(BF16)
+            return 0
+
+        lax.fori_loop(0, 4, one, 0)
+        stores = [
+            pltpu.make_async_copy(ewu_v, ewu_o, store_sem.at[0]),
+            pltpu.make_async_copy(ewd_v, ewd_o, store_sem.at[1]),
+        ]
+        for store in stores:
+            store.start()
+        return stores
+
     back = collect_z(0)
+    stores = expert_grads()
+    collect_forward(0, back)
+    back_copies = collect_plane(0, back)
     out = collect_z(1)
-    collect_forward(0, back)
+    grad_in = collect_last(0, back_copies)
+
+    def norm_back(rows, gain, grads):
+        hat, scale = normalise(rows)
+        weighted = grads * gain
+        back_rows = scale * (
+            weighted
+            - jnp.mean(weighted, axis=-1, keepdims=True)
+            - hat * jnp.mean(weighted * hat, axis=-1, keepdims=True)
+        )
+        return back_rows, jnp.sum(grads * hat, axis=0, keepdims=True) * dense_scale
+
+    back_hidden, gain_moe_term = norm_back(hidden_o[...], gain_m[...].reshape(1, 768), grad_in)
+    grad_hidden = gout[...].astype(F32) + back_hidden
+    gg_v[...] = grad_hidden
+    hidden_back = grad_hidden.astype(BF16)
+    hbx[c] = hidden_back
+    hb_copy = send(hbx.at[c], hbx.at[c], xs.at[3], xr.at[3], sib_dev)
+    conv = conv_o[...]
+    s = jax.nn.sigmoid(conv)
+    gc_pad[16:144] = (dot_nt(hidden_back, wout_v[...]) * (s + conv * s * (1.0 - s))).astype(BF16)
+    halo = [
+        send(gc_pad.at[128:144], gc_pad.at[0:16], halo_s.at[1, 0], halo_r.at[1, 0], next_dev),
+        send(gc_pad.at[16:32], gc_pad.at[144:160], halo_s.at[1, 1], halo_r.at[1, 1], prev_dev),
+    ]
+
+    axes = ("zyx", "yxz", "xzy", "zyx")
+    place = {"z": z, "y": y, "x": x}
+
+    def along(axis, offset):
+        if axis == "z":
+            return (lax.rem(z + offset, 4) * 2 + c, exp)
+        if axis == "y":
+            return (seq, lax.rem(y + offset, 4) * 4 + x)
+        return (seq, y * 4 + lax.rem(x + offset, 4))
+
+    def scatter(p, level, src, dst, ssem, rsem):
+        axis = axes[p][level]
+        copies = []
+        for i in range(3):
+            target = lax.rem(place[axis] + i + 1, 4)
+            copies.append(
+                send(src.at[target], dst.at[i], ssem.at[p, i], rsem.at[p, i], along(axis, i + 1))
+            )
+        return copies
+
+    def gathered(p, level, src, dst, copies):
+        for copy in copies:
+            copy.wait_recv()
+        total = src[place[axes[p][level]]].astype(F32)
+        for i in range(3):
+            total = total + dst[i].astype(F32)
+        return total
+
+    def buffers(p):
+        if p == 3:
+            return sax, rax, sbx, rbx, tdx, sdx, rdx
+        return tuple(ref.at[p] for ref in (sa, ra, sb, rb, td, sd, rdd))
+
+    def first_level(p, value):
+        src, dst = buffers(p)[0:2]
+        src[...] = value.astype(BF16).reshape(4, 96, value.shape[-1])
+        return scatter(p, 0, src, dst, ra_s, ra_r)
+
+    def second_level(p, copies):
+        src0, dst0, src, dst = buffers(p)[0:4]
+        total = gathered(p, 0, src0, dst0, copies)
+        pad = jnp.zeros((8, total.shape[-1]), F32)
+        for b in range(4):
+            src[b] = jnp.concatenate([total[24 * b : 24 * b + 24], pad], axis=0).astype(BF16)
+        return scatter(p, 1, src, dst, rb_s, rb_r)
+
+    def third_level(p, copies):
+        src0, dst0, flat, src, dst = buffers(p)[2:7]
+        flat[...] = gathered(p, 1, src0, dst0, copies)
+        for d in range(4):
+            src[d] = flat[6 * d : 6 * d + 8]
+        return scatter(p, 2, src, dst, rd_s, rd_r)
+
+    def last_level(p, copies):
+        return gathered(p, 2, *buffers(p)[5:7], copies)
+
     collect_forward(1, out)
-    back_copies = collect_plane(0, back)
-    gmi_o[...] = collect_last(0, back_copies)
+
+    terms_v[c] = jnp.zeros((40, 768), F32)
+    terms_v[c, 33:34] = gain_moe_term
+
+    def put_tap(k, cols, value):
+        terms_v[c, k : k + 1, cols] = value * dense_scale
+
+    tap_grads(shifted, gc_pad, put_tap)
+
+    chosen[2].wait_recv()
+    hb_copy.wait_recv()
+    part2 = dot_tn(ap[2].reshape(256, 384), hbx[...].reshape(256, 768)) * dense_scale
+    level2 = first_level(2, part2)
+
+    for copy in halo:
+        copy.wait_recv()
+
+    @pl.when(seq == 0)
+    def _():
+        gc_pad[0:16] = jnp.zeros((16, 768), BF16)
+
+    @pl.when(seq == 7)
+    def _():
+        gc_pad[144:160] = jnp.zeros((16, 768), BF16)
+
+    shift_copies(gc_pad, shifted_b)
+    conv_taps(shifted_b, dw, conv_o, True)
+    grad_glu = conv_o[...]
+    gate = jax.nn.sigmoid(mixed_o[:, 768:1536])
+    gmx[c, :, 0:768] = (grad_glu * gate).astype(BF16)
+    gmx[c, :, 768:1536] = (grad_glu * mixed_o[:, 0:768] * gate * (1.0 - gate)).astype(BF16)
+    gm_copy = send(gmx.at[c], gmx.at[c], xs.at[4], xr.at[4], sib_dev)
     out_copies = collect_plane(1, out)
-    eo_o[...] = collect_last(1, out_copies)
-    for l in range(4):
-        rows_o[l] = xp[1, l].reshape(512, 768)
-        grows_o[l] = xp[0, l].reshape(512, 768)
+    grad_normed = dot_nt(gmx[c], win_v[...])
+    back_source, gain_conv_term = norm_back(
+        frames[...].astype(F32), gain_c[...].reshape(1, 768), grad_normed
+    )
+    gx_o[...] = (gg_v[...] + back_source).astype(BF16)
+    terms_v[c, 32:33] = gain_conv_term
+    dx_copy = send(terms_v.at[c], terms_v.at[c], xs.at[5], xr.at[5], sib_dev)
+    gm_copy.wait_recv()
+    chosen[0].wait_recv()
+    chosen[1].wait_recv()
+    levels = [None, None, level2, None]
+    for p in range(2):
+        grads = gmx[:, :, 768 * p : 768 * (p + 1)].reshape(256, 768)
+        levels[p] = first_level(p, dot_tn(ap[p].reshape(256, 384), grads) * dense_scale)
+    dx_copy.wait_recv()
+    terms = (terms_v[0] + terms_v[1]).astype(BF16)
+    terms = jnp.concatenate([terms.astype(F32), jnp.zeros((88, 768), F32)], axis=0).astype(BF16)
+    levels[3] = first_level(3, dot_nt(row_choice(0, c), terms))
+    block_o[...] = (hidden_o[...] + 0.5 * collect_last(1, out_copies)).astype(BF16)
+    for p in (2, 0, 1, 3):
+        levels[p] = second_level(p, levels[p])
+    for p in (2, 0, 1, 3):
+        levels[p] = third_level(p, levels[p])
+    gwo_o[...] = last_level(2, levels[2])[0:6]
+    gwi_o[:, 0:768] = last_level(0, levels[0])[0:6]
+    gwi_o[:, 768:1536] = last_level(1, levels[1])[0:6]
+    ext_o[...] = last_level(3, levels[3])
+    for store in stores:
+        store.wait()
     for copy in sent:
         copy.wait_send()
 
@@ -395,14 +530,12 @@
         out_shape=[
             jax.ShapeDtypeStruct(shape, dtype)
             for shape, dtype in (
-                ((128, 768), F32), ((128, 768), F32), ((128, 768), F32), ((128, 768), F32),
-                ((160, 768), BF16), ((128, 1536), F32), ((128, 768), BF16), ((128, 768), BF16),
-                ((4, 512, 768), BF16), ((4, 512, 768), BF16),
-                ((4, 512, 384), BF16), ((4, 512, 384), BF16),
+                ((128, 768), BF16), ((128, 768), BF16), ((6, 1536), F32), ((6, 768), F32),
+                ((8, 128), F32), ((4, 768, 384), BF16), ((4, 384, 768), BF16),
             )
         ],
         in_specs=[vmem, vmem, any_spec, vmem, any_spec, vmem, any_spec, any_spec, vmem, vmem, vmem],
-        out_specs=[vmem] * 12,
+        out_specs=[vmem] * 5 + [any_spec] * 2,
         scratch_shapes=[
             pltpu.VMEM((768, 1536), BF16),
             pltpu.VMEM((768, 768), BF16),
@@ -422,9 +555,28 @@
             pltpu.VMEM((2, 4, 4, 16, 768), BF16),
             pltpu.VMEM((2, 4, 4, 16, 768), BF16),
             pltpu.VMEM((2, 4, 4, 16, 768), BF16),
-            dma((2, 16)), dma((2, 16)), dma((1, 2)), dma((1, 2)),
+            pltpu.VMEM((128, 768), F32), pltpu.VMEM((128, 768), F32),
+            pltpu.VMEM((160, 768), BF16), pltpu.VMEM((128, 1536), F32),
+            pltpu.VMEM((128, 768), BF16), pltpu.VMEM((128, 768), BF16),
+            pltpu.VMEM((4, 512, 384), BF16), pltpu.VMEM((4, 512, 384), BF16),
+            pltpu.VMEM((4, 768, 384), BF16), pltpu.VMEM((4, 384, 768), BF16),
+            pltpu.VMEM((160, 768), BF16), pltpu.VMEM((8, 160, 768), F32),
+            pltpu.VMEM((3, 2, 128, 384), BF16), pltpu.VMEM((3, 128, 384), BF16),
+            pltpu.VMEM((2, 128, 768), BF16), pltpu.VMEM((2, 128, 1536), BF16),
+            pltpu.VMEM((2, 40, 768), F32), pltpu.VMEM((128, 768), F32),
+            pltpu.VMEM((3, 4, 96, 768), BF16), pltpu.VMEM((3, 3, 96, 768), BF16),
+            pltpu.VMEM((3, 4, 32, 768), BF16), pltpu.VMEM((3, 3, 32, 768), BF16),
+            pltpu.VMEM((3, 32, 768), F32),
+            pltpu.VMEM((3, 4, 8, 768), F32), pltpu.VMEM((3, 3, 8, 768), F32),
+            pltpu.VMEM((4, 96, 128), BF16), pltpu.VMEM((3, 96, 128), BF16),
+            pltpu.VMEM((4, 32, 128), BF16), pltpu.VMEM((3, 32, 128), BF16),
+            pltpu.VMEM((32, 128), F32),
+            pltpu.VMEM((4, 8, 128), F32), pltpu.VMEM((3, 8, 128), F32),
+            dma((2, 16)), dma((2, 16)), dma((2, 2)), dma((2, 2)),
             dma((2, 2, 4)), dma((2, 2, 4)), dma((2, 4)), dma((2, 4)), dma((2, 4)), dma((2, 4)),
             dma((2, 4)), dma((2, 4)), dma((2, 6)), dma((2, 6)), dma((2, 16)), dma((2, 16)), dma((4,)),
+            dma((6,)), dma((6,)), dma((4, 3)), dma((4, 3)), dma((4, 3)), dma((4, 3)),
+            dma((4, 3)), dma((4, 3)), dma((2,)),
         ],
         compiler_params=pltpu.CompilerParams(
             collective_id=0, has_side_effects=True, vmem_limit_bytes=62 * 1024 * 1024
@@ -435,103 +587,20 @@
 def per_device(
     frames_in, gain_conv, w_in, dw_kernel, w_out, gain_moe, w_up, w_down, route, slot, grad_out
 ):
-    seq_count = lax.axis_size("seq")
-    exp_count = lax.axis_size("exp")
-    length = frames_in.shape[1]
-    feat_width = frames_in.shape[2]
-    local_experts = w_up.shape[0]
-    capacity = 2 * length // (local_experts * exp_count)
-    slot_count = local_experts * exp_count * capacity
-    tap_count = dw_kernel.shape[0]
-    half_kernel = tap_count // 2
-    dense_scale = (length * seq_count * exp_count) ** (-0.5)
-    expert_scale = (seq_count * exp_count * capacity) ** (-0.5)
-    source = frames_in[0].astype(jnp.float32)
-    (
-        expert_out, grad_moe_in, hidden, conv_out, glu_rows, mixed_cols, normed, act_out,
-        expert_rows, grad_rows, up_act, grad_pre,
-    ) = run_fused(
-        frames_in[0], gain_conv[None], w_in, dw_kernel, w_out, gain_moe[None], w_up, w_down,
+    block_out, grad_x, grad_w_in, grad_w_out, terms, grad_w_up, grad_w_down = run_fused(
+        frames_in[0], gain_conv, w_in, dw_kernel, w_out, gain_moe, w_up, w_down,
         route, slot, grad_out[0],
-    )
-    glu_pad = glu_rows[1:159]
-    block_out = (hidden + 0.5 * expert_out).astype(jnp.bfloat16)
-    grad_w_down = (
-        jnp.einsum("erf,erd->efd", up_act, grad_rows, preferred_element_type=jnp.float32)
-        * expert_scale
-    )
-    grad_w_up = (
-        jnp.einsum("erd,erf->edf", expert_rows, grad_pre, preferred_element_type=jnp.float32)
-        * expert_scale
-    )
-    _, pull_back = jax.vjp(layer_norm, hidden, gain_moe)
-    back_hidden, gain_moe_term = pull_back(grad_moe_in)
-    grad_hidden = grad_out[0].astype(jnp.float32) + back_hidden
-    hidden_back = grad_hidden.astype(jnp.bfloat16)
-    grad_w_out = (
-        jnp.einsum("ld,le->de", act_out, hidden_back, preferred_element_type=jnp.float32)
-        * dense_scale
-    )
-    grad_conv = (
-        jnp.einsum("le,de->ld", hidden_back, w_out, preferred_element_type=jnp.float32)
-        * swish_slope(conv_out)
-    ).astype(jnp.bfloat16)
-    conv_pad = extended(grad_conv, (("seq", 0),), half_kernel)
-    grad_glu = depthwise(conv_pad, dw_kernel[::-1], length)
-    grad_dw = tap_sums(glu_pad, grad_conv.astype(jnp.float32), length, tap_count) * dense_scale
-    _, pull_glu = jax.vjp(gated_linear, mixed_cols)
-    grad_mixed = pull_glu(grad_glu)[0].astype(jnp.bfloat16)
-    grad_w_in = (
-        jnp.einsum("ld,le->de", normed, grad_mixed, preferred_element_type=jnp.float32)
-        * dense_scale
-    )
-    grad_normed = jnp.einsum("le,de->ld", grad_mixed, w_in, preferred_element_type=jnp.float32)
-    _, pull_input = jax.vjp(layer_norm, source, gain_conv)
-    back_source, gain_conv_term = pull_input(grad_normed)
-    grad_x = (grad_hidden + back_source).astype(jnp.bfloat16)
-    devices = seq_count * exp_count
-
-    def by_rows(value):
-        return value.reshape(devices, -1)
-
-    sent = jnp.concatenate(
-        [
-            by_rows(grad_w_in),
-            by_rows(grad_w_out),
-            by_rows(grad_dw.T),
-            by_rows(gain_conv_term * dense_scale),
-            by_rows(gain_moe_term * dense_scale),
-        ],
-        axis=1,
-    ).astype(jnp.bfloat16)
-    width = sent.shape[1]
-    tile_rows = -(-width // 2048) * 16
-    sent = jnp.pad(sent, ((0, 0), (0, tile_rows * 128 - width))).reshape(devices, tile_rows, 128)
-    came = lax.all_to_all(sent, ("seq", "exp"), split_axis=0, concat_axis=0, tiled=True)
-    total = jnp.sum(came.astype(jnp.float32), axis=0).reshape(-1)
-    own = feat_width // devices
-    sizes = (own * 2 * feat_width, own * feat_width, own * tap_count, own, own)
-    parts, start = [], 0
-    for size in sizes:
-        parts.append(total[start : start + size])
-        start += size
-    shared = (
-        parts[0].reshape(own, 2 * feat_width),
-        parts[2].reshape(own, tap_count).T,
-        parts[1].reshape(own, feat_width),
-        parts[3],
-        parts[4],
     )
     return (
         block_out[None],
         grad_x[None],
-        shared[0],
-        shared[1],
-        shared[2],
-        shared[3],
-        shared[4],
-        grad_w_up,
-        grad_w_down,
+        grad_w_in,
+        terms[0:6, 0:31].T,
+        grad_w_out,
+        terms[0:6, 32],
+        terms[0:6, 33],
+        grad_w_up.astype(jnp.float32),
+        grad_w_down.astype(jnp.float32),
     )
 
 

time: 215 us -> 123 us (0.57)
  waiting for transfers between devices: 35.3 us -> 0 us
  local copies, waits for them, and re-layouts: 32 us -> 5.35 us
  matrix products: 16.7 us -> 0 us
  starting transfers between devices: 12 us -> 0 us
  other arithmetic: 18 us -> 6.9 us
  Pallas kernels: 98.6 us -> 109 us
    all_to_all x1 -> x0, waiting for transfers between devices: 35.3 us -> none  [per_device(): lax.all_to_all(sent, ('seq', 'exp'), split_axis=0, concat_axis=0, tiled=T...]
    dot_general x6 -> x0, matrix products: 16.7 us -> none  [the longest x1 6.07 us: per_device(): jnp.einsum('erd,erf->edf', expert_rows, grad_pre, preferred_element_type=...]
    pallas_call x1, Pallas kernels: 98.6 us -> 109 us  [run_fused(): pl.pallas_call(fused_kernel, out_shape=[jax.ShapeDtypeStruct(shape, dtype...]
    reshape x6 -> x0, local copies, waits for them, and re-layouts: 10.1 us -> none  [the longest x3 8.17 us: by_rows(): return value.reshape(devices, -1)]
    reduce_sum x8 -> x0, other arithmetic: 9.65 us -> none  [the longest x3 3.43 us: layer_norm(): centre = frame_rows - jnp.mean(frame_rows, axis=-1, keepdims=True)]
    all_to_all x1 -> x0, starting transfers between devices: 6.94 us -> none  [per_device(): lax.all_to_all(sent, ('seq', 'exp'), split_axis=0, concat_axis=0, tiled=T...]
    convert_element_type x1 -> x2, other arithmetic: 0.11 us -> 6.9 us  [the longest x1 4.3 us: per_device(): grad_w_up.astype(jnp.float32)]
    concatenate x1 -> x0, local copies, waits for them, and re-layouts: 5.96 us -> none  [per_device(): jnp.concatenate([by_rows(grad_w_in), by_rows(grad_w_out), by_rows(grad_dw...]
  transfers between devices with their start and end apart: 3 -> 0, of which waited for: 1 -> 0; matrix products, arithmetic and copies ran while one was open for 11% -> 0% of each run, Pallas kernels for 0% -> 0%
where the time goes in v3:
time: 123 us; the launch traced here: 122 us
  Pallas kernels  109 us (89%)
  other arithmetic  6.9 us (6%)
  local copies, waits for them, and re-layouts  5.35 us (4%)
    pallas_call x1, Pallas kernels, run_fused(): pl.pallas_call(fused_kernel, out_shape=[jax.ShapeDtypeStruct(shape, dtype...  109 us
    convert_element_type x1, other arithmetic, per_device(): grad_w_up.astype(jnp.float32)  4.3 us
    unnamed x14, local copies, waits for them, and re-layouts  2.6 us
    convert_element_type x1, other arithmetic, per_device(): grad_w_down.astype(jnp.float32)  2.59 us

profile of v3, /device:TPU:1, one launch (start us, length us, event | category | flops | bytes accessed | tf_op | source)
XLA Modules:
  0.0 121.7 jit_solution(2846909077825682461)
XLA Ops:
  0.6 108.7 %shard_map.178 = (bf16[128,768]{1,0:T(8,128)(2,1)}, bf16[128,768]{1,0:T(8,128)(2,1)}, f32[6,1536]{1,0:T(8,128)}, f32[6,768]{1,0:T(8,128)}, f32[8,128]{1,0:T(8,12...) custom-call(bf16[128,768]{1,0:T(8,128)(2,1)} %bitcast.8, f32[768]{0:T(1024)} %gain_c.1, ...), custom_call_target="tpu_custom_call" | custom-call | tf_op jit(solution)/shard_map/pallas_call | solution.py:528
  109.4 1.5 %slice_reduce_fusion = (f32[6]{0:T(128)}, f32[6]{0:T(128)}) fusion(f32[8,128]{1,0:T(8,128)} %get-tuple-element.19), kind=kLoop, calls=%fused_computation | loop fusion | bytes 96 | tf_op jit(solution)/shard_map/slice | solution.py:601
  110.9 1.3 %slice_bitcast_fusion = f32[31,6]{0,1:T(8,128)} fusion(f32[8,128]{1,0:T(8,128)} %get-tuple-element.19), kind=kLoop, calls=%fused_computation.2 | loop fusion | bytes 1488 | tf_op jit(solution)/shard_map/transpose | solution.py:598
  112.1 0.0 copy-start
  112.1 4.3 %convert_element_type.6 = f32[4,768,384]{2,1,0:T(8,128)} convert(bf16[4,768,384]{2,1,0:T(8,128)(2,1)} %get-tuple-element.21) | non-fusion elementwise | flops 1179648 | bytes 7077888 | tf_op jit(solution)/shard_map/convert_element_type | solution.py:602
  116.4 0.0 copy-done
  116.4 0.0 copy-start.2
  116.4 0.0 copy-start.1
  116.4 0.0 copy-start.3
  116.5 0.0 copy-start.4
  116.5 2.6 %convert_element_type.7 = f32[4,384,768]{2,1,0:T(8,128)} convert(bf16[4,384,768]{2,1,0:T(8,128)(2,1)S(1)} %copy-done) | non-fusion elementwise | flops 1179648 | bytes 7077888 | tf_op jit(solution)/shard_map/convert_element_type | solution.py:603
  119.1 0.0 copy-done.2
  119.1 0.7 copy.24
  119.7 0.0 copy-done.1
  119.7 0.7 copy.25
  120.4 0.0 copy-done.3
  120.4 0.6 copy.26
  121.0 0.0 copy-done.4
  121.0 0.6 copy.27
Async XLA Ops:
  112.1 4.3 %copy-start = (bf16[4,384,768]{2,1,0:T(8,128)(2,1)S(1)}, bf16[4,384,768]{2,1,0:T(8,128)(2,1)}, u32[]{:S(2)}) copy-start(bf16[4,384,768]{2,1,0:T(8,128)(2,1)} %get-tuple-element.22) | copy-start | bytes 7077892
  116.4 2.6 %copy-start.2 = (bf16[128,768]{1,0:T(8,128)(2,1)S(1)}, bf16[128,768]{1,0:T(8,128)(2,1)}, u32[]{:S(2)}) copy-start(bf16[128,768]{1,0:T(8,128)(2,1)} %get-tuple-element.16) | copy-start | bytes 589828
  116.4 3.3 %copy-start.1 = (bf16[128,768]{1,0:T(8,128)(2,1)S(1)}, bf16[128,768]{1,0:T(8,128)(2,1)}, u32[]{:S(2)}) copy-start(bf16[128,768]{1,0:T(8,128)(2,1)} %get-tuple-element.17) | copy-start | bytes 589828
  116.4 4.0 %copy-start.3 = (f32[6,1536]{1,0:T(8,128)S(1)}, f32[6,1536]{1,0:T(8,128)}, u32[]{:S(2)}) copy-start(f32[6,1536]{1,0:T(8,128)} %get-tuple-element.36) | copy-start | bytes 110596
  116.5 4.6 %copy-start.4 = (f32[6,768]{1,0:T(8,128)S(1)}, f32[6,768]{1,0:T(8,128)}, u32[]{:S(2)}) copy-start(f32[6,768]{1,0:T(8,128)} %get-tuple-element.38) | copy-start | bytes 55300
